TPU v7x, 128 devices: a whole 4x4x4 slice. The times are simulated.
128 devices in a mesh: gx: 4 (over x_hi, core), dev: 32 (over z, y, x_lo).
Axes of the slice: x: 4 (x_hi: 2, x_lo: 2; x = x_hi * 2 + x_lo), y: 4, z: 4, core: 2. Of those that a mesh axis runs over, the one named last changes fastest.
Arguments:
- volume: float32 [64, 128, 4096], P('gx', 'dev'), may hold values from -60 to 60
- occupancy: int32 [8, 32], P('gx', 'dev'), may hold values 0 or 1
Outputs:
- structure: float32 [6, 64, 128, 4096], P(None, 'gx', 'dev')
All inputs are finite; a program needn't handle non-finite values. No bound on the sum of `occupancy` on one device may be relied on, other than what follows from the above.
Results may differ from a plain program's by a relative error of at most 0.00002.
Values sent between devices are 32-bit elements; how exact they have to be, the bound alone decides.
No kernel may reach another device: no remote copies, remote signals or barrier semaphores. Data moves between devices by JAX's collectives and lax.ppermute only.
A program may use at most 256 MiB of HBM per device.

v0:
```python
import math

import jax
import jax.numpy as jnp
from jax import lax
from jax.sharding import PartitionSpec as P

RAD_D = 3
RAD_S = 12
BRICK_X = 8
BRICK_Z = 4


SIGMA_DERIV = 1.0
SIGMA_SMOOTH = 4.0


def extended_2(x, sides, width):
    for axis, dim in sides:
        size, length = (lax.axis_size(axis), x.shape[dim])
        up = [(i, (i + 1) % size) for i in range(size - 1)]
        down = [(j, i) for i, j in up]
        last = lax.slice_in_dim(x, length - width, length, axis=dim)
        first = lax.slice_in_dim(x, 0, width, axis=dim)
        before = lax.ppermute(last, axis, up)
        after = lax.ppermute(first, axis, down)
        x = jnp.concatenate([before, x, after], axis=dim)
    return x


def kernel_taps(radius, width_sigma, derivative):
    offsets = [float(t) for t in range(-radius, radius + 1)]
    weights = [math.exp(-0.5 * (t / width_sigma) ** 2) for t in offsets]
    if derivative:
        total = sum((t * t * w for t, w in zip(offsets, weights)))
        return [t * w / total for t, w in zip(offsets, weights)]
    total = sum(weights)
    return [w / total for w in weights]


def line_pass(source, weights, dimension):
    length_out = source.shape[dimension] - len(weights) + 1
    summed = float(weights[0]) * lax.slice_in_dim(source, 0, length_out, axis=dimension)
    for offset in range(1, len(weights)):
        summed = summed + float(weights[offset]) * lax.slice_in_dim(
            source, offset, offset + length_out, axis=dimension
        )
    return summed


def pad_dimension(source, dimension, radius):
    widths = [(0, 0)] * source.ndim
    widths[dimension] = (radius, radius)
    return jnp.pad(source, widths)


def on_device(volume, occupancy):
    smooth_d = kernel_taps(RAD_D, SIGMA_DERIV, False)
    deriv_d = kernel_taps(RAD_D, SIGMA_DERIV, True)
    smooth_s = kernel_taps(RAD_S, SIGMA_SMOOTH, False)
    presence = jnp.repeat(jnp.repeat(occupancy, BRICK_X, 0), BRICK_Z, 1).astype(jnp.float32)
    masked = (volume * presence[:, :, None])[None]
    upright = lax.all_to_all(masked, "dev", split_axis=3, concat_axis=2, tiled=True)
    padded = pad_dimension(upright, 2, RAD_D)
    paired = jnp.concatenate([line_pass(padded, smooth_d, 2), line_pass(padded, deriv_d, 2)], 0)
    paired = lax.all_to_all(paired, "dev", split_axis=2, concat_axis=3, tiled=True)
    extended = extended_2(paired, (("gx", 1),), RAD_D)
    extended = pad_dimension(extended, 3, RAD_D)
    smooth_a = line_pass(extended[0], smooth_d, 2)
    deriv_a = line_pass(extended[0], deriv_d, 2)
    smooth_b = line_pass(extended[1], smooth_d, 2)
    grad_x = line_pass(smooth_a, deriv_d, 0)
    grad_y = line_pass(deriv_a, smooth_d, 0)
    grad_z = line_pass(smooth_b, smooth_d, 0)
    tensor = jnp.stack(
        [
            grad_x * grad_x,
            grad_x * grad_y,
            grad_x * grad_z,
            grad_y * grad_y,
            grad_y * grad_z,
            grad_z * grad_z,
        ],
        0,
    )
    tensor = extended_2(tensor, (("gx", 1),), RAD_S)
    tensor = pad_dimension(tensor, 3, RAD_S)
    tensor = line_pass(line_pass(tensor, smooth_s, 3), smooth_s, 1)
    tensor = lax.all_to_all(tensor, "dev", split_axis=3, concat_axis=2, tiled=True)
    tensor = line_pass(pad_dimension(tensor, 2, RAD_S), smooth_s, 2)
    return lax.all_to_all(tensor, "dev", split_axis=2, concat_axis=3, tiled=True)


def solution(mesh):
    return jax.shard_map(
        on_device,
        mesh=mesh,
        in_specs=(P("gx", "dev", None), P("gx", "dev")),
        out_specs=P(None, "gx", "dev", None),
        check_vma=False,
    )
```

profile of v0, /device:TPU:1, one launch (start us, length us, event | category | flops | bytes accessed | tf_op | source)
XLA Modules:
  0.0 839.5 jit_solution(11253628782339124558)
XLA Ops:
  0.0 0.7 convert_bitcast_fusion
  0.8 7.0 copy.24
  7.8 7.5 fusion.123
  15.2 8.1 reshape.39
  23.4 26.3 %all_to_all.72 = f32[32,1,8192]{2,1,0:T(1,128)S(1)} all-to-all(f32[32,1,8192]{2,1,0:T(1,128)S(1)} %reshape.39), channel_id=1, replica_groups=mesh['gx'=4,'dev'=32] {'dev'}, dimensions={0} | all-to-all | bytes 2097152 | tf_op jit(solution)/shard_map/all_to_all | solution.py:63
  49.7 0.5 broadcast.300
  50.3 3.2 reduce
  53.5 7.3 reshape.40
  60.7 6.8 copy.25
  67.5 0.6 copy.26
  68.1 0.8 multiply_add_fusion.4
  69.1 0.3 copy.27
  69.4 30.4 %all_to_all.73 = f32[2,16,128,128]{3,1,0,2:T(8,128)S(1)} all-to-all(f32[2,16,128,128]{3,1,0,2:T(8,128)S(1)} %copy.27), channel_id=1, replica_groups=mesh['gx'=4,'dev'=32] {'dev'}, dimensions={2} | all-to-all | bytes 4194304 | tf_op jit(solution)/shard_map/all_to_all | solution.py:66
  99.8 2.5 copy.46
  102.3 1.7 all_to_all.59
  104.3 7.4 collective-permute-start
  111.7 2.1 collective-permute-start.1
  113.8 4.0 collective-permute-done
  117.8 5.9 collective-permute-done.1
  123.7 1.5 select_maximum_fusion
  125.4 2.5 fusion.94
  127.9 2.6 multiply_add_fusion.1
  130.5 0.9 bitcast_dynamic-update-slice_fusion.5
  131.4 0.9 bitcast_dynamic-update-slice_fusion.4
  132.3 0.9 bitcast_dynamic-update-slice_fusion.3
  133.4 6.0 fusion.121
  139.5 6.0 copy.30
  145.5 2.3 collective-permute-start.3
  147.8 5.2 copy.29
  153.0 5.1 collective-permute-start.2
  158.2 44.2 %collective-permute-done.3 = f32[6,12,4,4096]{3,2,1,0:T(4,128)S(1)} collective-permute-done((f32[6,12,4,4096]{3,2,1,0:T(4,128)S(1)}, f32[6,12,4,4096]{3,2,1,0:T(4,128)S(1)}, u32[]{:S(2)}, u32[]{:S(2)}) %collective-permute-start.3) | collective-permute-done | bytes 4718624 | tf_op jit(solution)/shard_map/ppermute | solution.py:26
  202.4 2.8 copy.32
  205.2 4.4 collective-permute-done.2
  209.5 2.8 copy.31
  212.3 6.3 pad_maximum_fusion
  218.6 161.8 %multiply_add_fusion = f32[6,40,4,4096]{3,1,2,0:T(8,128)} fusion(f32[6,40,4,4096]{3,1,2,0:T(8,128)} %pad_maximum_fusion), kind=kLoop, calls=%fused_computation.1 | loop fusion | flops 192675840 | bytes 31457280 | tf_op jit(solution)/shard_map/add | solution.py:45
  380.5 81.2 %fusion.69 = f32[6,16,4,4096]{3,1,2,0:T(8,128)} fusion(f32[6,40,4,4096]{3,1,2,0:T(8,128)} %multiply_add_fusion), kind=kLoop, calls=%fused_computation.108 | loop fusion | flops 77070336 | bytes 163577856 | tf_op jit(solution)/shard_map/add | solution.py:45
  461.7 37.2 %copy.33 = f32[6,16,4,4096]{1,2,0,3:T(4,128)} copy(f32[6,16,4,4096]{3,1,2,0:T(8,128)} %fusion.69) | data formatting | bytes 12582912 | tf_op jit(solution)/shard_map/add | solution.py:45
  498.9 45.4 %reshape.41 = f32[32,1,49152]{2,1,0:T(1,128)} reshape(f32[4096,6,4,16]{3,2,1,0:T(4,128)} %bitcast.49) | data formatting | bytes 12582912
  544.3 45.7 %all_to_all.74 = f32[32,1,49152]{2,1,0:T(1,128)} all-to-all(f32[32,1,49152]{2,1,0:T(1,128)} %reshape.41), channel_id=1, replica_groups=mesh['gx'=4,'dev'=32] {'dev'}, dimensions={0} | all-to-all | bytes 12582912 | tf_op jit(solution)/shard_map/all_to_all | solution.py:89
  590.0 19.5 %reduce.1 = f32[32,49152]{1,0:T(8,128)} reduce(f32[32,1,49152]{2,1,0:T(1,128)} %all_to_all.74, f32[]{:T(128)} %broadcast.300), dimensions={1}, to_apply=%all_to_all.60.reduce_sub_computation | reduce | bytes 12582916 | tf_op jit(solution)/shard_map/all_to_all | solution.py:89
  609.4 58.8 %reshape.42 = f32[4096,6,4,16]{3,2,1,0:T(4,128)} reshape(f32[32,49152]{1,0:T(8,128)} %reduce.1) | data formatting | bytes 12582912
  668.2 38.9 %copy.41 = f32[6,16,4,32,128]{4,1,2,3,0:T(8,128)} copy(f32[6,16,4,32,128]{1,2,0,4,3:T(4,128)} %bitcast.50) | data formatting | bytes 12582912 | tf_op jit(solution)/shard_map/all_to_all | solution.py:89
  707.1 70.1 %fusion.68 = f32[6,16,128,128]{3,1,2,0:T(8,128)} fusion(f32[6,16,128,128]{3,1,2,0:T(8,128)} %bitcast.52), kind=kLoop, calls=%fused_computation.106 | loop fusion | flops 77070336 | bytes 12582912 | tf_op jit(solution)/shard_map/add | solution.py:45
  777.2 3.7 copy.36
  781.0 44.2 %all_to_all.75 = f32[6,16,128,128]{3,1,0,2:T(8,128)S(1)} all-to-all(f32[6,16,128,128]{3,1,0,2:T(8,128)S(1)} %copy.36), channel_id=1, replica_groups=mesh['gx'=4,'dev'=32] {'dev'}, dimensions={2} | all-to-all | bytes 12582912 | tf_op jit(solution)/shard_map/all_to_all | solution.py:91
  825.2 6.3 copy.43
  831.5 7.6 reshape.38
  (10 shorter events, 1.0 us)
Async XLA Ops:
  104.3 13.5 %collective-permute-start = (f32[2,3,4,4096]{3,1,2,0:T(4,128)S(1)}, f32[2,3,4,4096]{3,1,2,0:T(4,128)S(1)}, u32[]{:S(2)}, u32[]{:S(2)}) collective-permute-start(f32[2,3,4,4096]{3,1,2,0:T(4,128)S(1)} %get-tuple-element.15), channel_id=1, source_target_pairs={{0,32},{32,64},{64,96},{1,33},{33,65},{65,97},{2,34},{34,66},{66,9... | collective-permute-start | bytes 1179656 | tf_op jit(solution)/shard_map/ppermute | solution.py:25
  111.7 12.0 %collective-permute-start.1 = (f32[2,3,4,4096]{3,1,2,0:T(4,128)S(1)}, f32[2,3,4,4096]{3,1,2,0:T(4,128)S(1)}, u32[]{:S(2)}, u32[]{:S(2)}) collective-permute-start(f32[2,3,4,4096]{3,1,2,0:T(4,128)S(1)} %get-tuple-element.16), channel_id=1, source_target_pairs={{32,0},{64,32},{96,64},{33,1},{65,33},{97,65},{34,2},{66,34},{98,6... | collective-permute-start | bytes 1179656 | tf_op jit(solution)/shard_map/ppermute | solution.py:26
  139.5 8.3 copy-start
  145.5 56.9 %collective-permute-start.3 = (f32[6,12,4,4096]{3,2,1,0:T(4,128)S(1)}, f32[6,12,4,4096]{3,2,1,0:T(4,128)S(1)}, u32[]{:S(2)}, u32[]{:S(2)}) collective-permute-start(f32[6,12,4,4096]{3,2,1,0:T(4,128)S(1)} %copy.30), channel_id=1, source_target_pairs={{32,0},{64,32},{96,64},{33,1},{65,33},{97,65},{34,2},{66,34},{98,6... | collective-permute-start | bytes 14155784 | tf_op jit(solution)/shard_map/ppermute | solution.py:26
  153.0 56.5 %collective-permute-start.2 = (f32[6,12,4,4096]{3,2,1,0:T(4,128)}, f32[6,12,4,4096]{3,2,1,0:T(4,128)S(1)}, u32[]{:S(2)}, u32[]{:S(2)}) collective-permute-start(f32[6,12,4,4096]{3,2,1,0:T(4,128)} %copy.29), channel_id=1, source_target_pairs={{0,32},{32,64},{64,96},{1,33},{33,65},{65,97},{2,34},{34,66},{66,9... | collective-permute-start | bytes 14155784 | tf_op jit(solution)/shard_map/ppermute | solution.py:25
where the time goes:
time: 854 us; the launch traced here: 840 us
  other arithmetic  361 us (42%)
  local copies, waits for them, and re-layouts  256 us (30%)
  blocking collectives  147 us (17%)
  waiting for transfers between devices  58.5 us (7%)
  starting transfers between devices  17 us (2%)
    add x6, other arithmetic, line_pass(): summed + float(weights[offset]) * lax.slice_in_dim(source, offset, offset...  319 us
    unnamed x7, local copies, waits for them, and re-layouts  127 us
    ppermute x2, waiting for transfers between devices, extended_2(): after = lax.ppermute(first, axis, down)  50.1 us
    all_to_all x1, blocking collectives, on_device(): lax.all_to_all(tensor, 'dev', split_axis=3, concat_axis=2, tiled=True)  45.7 us
    all_to_all x1, blocking collectives, on_device(): lax.all_to_all(tensor, 'dev', split_axis=2, concat_axis=3, tiled=True)  44.2 us
    add x2, local copies, waits for them, and re-layouts, line_pass(): summed + float(weights[offset]) * lax.slice_in_dim(source, offset, offset...  40.9 us
    all_to_all x1, local copies, waits for them, and re-layouts, on_device(): lax.all_to_all(tensor, 'dev', split_axis=3, concat_axis=2, tiled=True)  38.9 us
    all_to_all x1, blocking collectives, on_device(): lax.all_to_all(paired, 'dev', split_axis=2, concat_axis=3, tiled=True)  30.4 us
  transfers between devices with their start and end apart: 4, of which 4 were waited for; matrix products, arithmetic and copies ran while one was open for 1% of the time, Pallas kernels for 0%

commit v1 on v0

v1 whole, which is shorter than its diff:
```python
import math

import jax
import jax.numpy as jnp
import ml_dtypes
import numpy as np
from jax import lax
from jax.experimental import pallas as pl
from jax.experimental.pallas import tpu as pltpu
from jax.sharding import PartitionSpec as P

RAD_D = 3
RAD_S = 12
SIGMA_DERIV = 1.0
SIGMA_SMOOTH = 4.0

NB = 32
LANES = 128
HALO_SLOT = 16
MSG_ROWS = 72
F32 = jnp.float32
BF16 = jnp.bfloat16


def kernel_taps(radius, width_sigma, derivative):
    offsets = [float(t) for t in range(-radius, radius + 1)]
    weights = [math.exp(-0.5 * (t / width_sigma) ** 2) for t in offsets]
    if derivative:
        total = sum((t * t * w for t, w in zip(offsets, weights)))
        return [t * w / total for t, w in zip(offsets, weights)]
    total = sum(weights)
    return [w / total for w in weights]


G1 = kernel_taps(RAD_D, SIGMA_DERIV, False)
D1 = kernel_taps(RAD_D, SIGMA_DERIV, True)
G4 = kernel_taps(RAD_S, SIGMA_SMOOTH, False)


def halves(matrix):
    high = matrix.astype(ml_dtypes.bfloat16)
    low = (matrix - high.astype(np.float64)).astype(ml_dtypes.bfloat16)
    return high, low


def band(taps, n):
    radius = len(taps) // 2
    m = np.zeros((n, n))
    for i in range(n):
        for t in range(-radius, radius + 1):
            if 0 <= i + t < n:
                m[i, i + t] = taps[t + radius]
    return m


def y_gradient_matrix():
    m = np.zeros((2 * LANES, 2 * LANES))
    for part, taps in enumerate((G1, D1)):
        for y in range(LANES):
            for t in range(-RAD_D, RAD_D + 1):
                s = y + t
                w = taps[t + RAD_D]
                col = part * LANES + y
                if 0 <= s < LANES:
                    m[s, col] = w
                else:
                    k = s + RAD_D if s < 0 else RAD_D + s - LANES
                    for seg in range(8):
                        m[LANES + seg * HALO_SLOT + k, col] = w
    return m


def pair_order():
    return [(xp, 4 * d + z) for d in range(NB) for xp in range(2) for z in range(4)]


def z_gradient_matrix():
    smooth, deriv = band(G1, 128), band(D1, 128)
    m = np.zeros((512, 256))
    for col, (xp, z) in enumerate(pair_order()):
        m[xp * 128 : xp * 128 + 128, col] = smooth[:, z]
        m[256 + xp * 128 : 256 + xp * 128 + 128, col] = deriv[:, z]
    return m


def z_smooth_matrix():
    smooth = band(G4, 128)
    m = np.zeros((256, 256))
    for row, (xp, z) in enumerate(pair_order()):
        m[row, xp * 128 : xp * 128 + 128] = smooth[z]
    return m


def y_smooth_matrix():
    m = np.zeros((384, 256))
    for y in range(256):
        for t in range(-RAD_S, RAD_S + 1):
            s = y + t
            if s < 0:
                s = 256 + 128 + s
            elif s >= 256:
                s = 256 + s - 256
            m[s, y] = G4[t + RAD_S]
    return m


def split(x):
    high = x.astype(BF16)
    return high, (x - high.astype(F32)).astype(BF16)


def dot(a, b):
    return jnp.dot(a, b, preferred_element_type=F32)


def pack_kernel(occ_ref, vol_ref, out_ref):
    lane = lax.broadcasted_iota(jnp.int32, (8, LANES), 1)
    for p in range(8):
        present = occ_ref[p // 4, 0].astype(F32)
        rows = jnp.concatenate([vol_ref[2 * p], vol_ref[2 * p + 1]], axis=0) * present
        blocks = [rows[:, j * LANES : (j + 1) * LANES] for j in range(NB)]
        zero = jnp.zeros((8, LANES), F32)
        for j in range(NB):
            out_ref[j, 8 * p : 8 * p + 8, :] = blocks[j]
            before = blocks[j - 1] if j > 0 else zero
            after = blocks[j + 1] if j < NB - 1 else zero
            rim = jnp.where(lane >= LANES - 3, before, jnp.where(lane < 3, after, 0.0))
            rim = pltpu.roll(rim, 3, 1, stride=HALO_SLOT, stride_axis=0)
            out_ref[j, 64 + p, :] = jnp.sum(rim, axis=0)


def pack(volume, occupancy):
    return pl.pallas_call(
        pack_kernel,
        out_shape=jax.ShapeDtypeStruct((NB, MSG_ROWS, LANES), F32),
        in_specs=[
            pl.BlockSpec(memory_space=pltpu.SMEM),
            pl.BlockSpec(memory_space=pltpu.VMEM),
        ],
        out_specs=pl.BlockSpec(memory_space=pltpu.VMEM),
        name="pack",
    )(occupancy, volume)


NROW = 48
PROWS = 40


def tensor_kernel(
    edge_ref, left_ref, own_ref, right_ref, gh_ref, gl_ref, wh_ref, wl_ref, bh_ref, bl_ref,
    out_ref, fields, prods, sums,
):
    row = lax.broadcasted_iota(jnp.int32, (8, LANES), 0)
    lane = lax.broadcasted_iota(jnp.int32, (8, LANES), 1)
    mine = (row == lane // HALO_SLOT)[None]

    for part, src in enumerate((left_ref, own_ref, right_ref)):

        def pair(p, carry, part=part, src=src):
            first = pl.multiple_of(8 * p, 8)
            main = src[:, pl.ds(first, 8), :].reshape(256, LANES)
            rim = src[:, pl.ds(64 + p, 1), :]
            rim = jnp.where(mine, jnp.broadcast_to(rim, (NB, 8, LANES)), 0.0)
            xh, xl = split(jnp.concatenate([main, rim.reshape(256, LANES)], axis=1))
            y = dot(xh, gh_ref[...]) + dot(xl, gh_ref[...]) + dot(xh, gl_ref[...])
            yh, yl = split(y)
            smooth = (
                dot(wh_ref[:256, :], yh) + dot(wh_ref[:256, :], yl) + dot(wl_ref[:256, :], yh)
            )
            ah, al = yh[:, :LANES], yl[:, :LANES]
            deriv = dot(wh_ref[256:, :], ah) + dot(wh_ref[256:, :], al) + dot(wl_ref[256:, :], ah)
            e = 16 * part + 2 * p
            fields[0, pl.ds(e, 2)] = smooth[:, :LANES].reshape(2, 128, LANES)
            fields[1, pl.ds(e, 2)] = smooth[:, LANES:].reshape(2, 128, LANES)
            fields[2, pl.ds(e, 2)] = deriv.reshape(2, 128, LANES)
            return carry

        lax.fori_loop(0, 8, pair, 0)

    def product_row(r, carry):
        keep = jnp.where((r < 12) & (edge_ref[0] == 0), 0.0, 1.0)
        keep = jnp.where((r >= 28) & (edge_ref[0] == 3), 0.0, keep)
        for zt in range(16):
            rows = pl.ds(8 * zt, 8)

            def tap(f, t):
                return fields[f, r + (4 + t), rows, :]

            def sym(f):
                s = G1[3] * tap(f, 0)
                for t in (1, 2, 3):
                    s = s + G1[3 + t] * (tap(f, t) + tap(f, -t))
                return s * keep

            gx = D1[4] * (tap(0, 1) - tap(0, -1))
            for t in (2, 3):
                gx = gx + D1[3 + t] * (tap(0, t) - tap(0, -t))
            gx = gx * keep
            gy = sym(1)
            gz = sym(2)
            prods[0, r, rows, :] = gx * gx
            prods[1, r, rows, :] = gx * gy
            prods[2, r, rows, :] = gx * gz
            prods[3, r, rows, :] = gy * gy
            prods[4, r, rows, :] = gy * gz
            prods[5, r, rows, :] = gz * gz
        return carry

    lax.fori_loop(0, PROWS, product_row, 0)

    def smooth_x(i, carry):
        c = i // 16
        rows = pl.ds(pl.multiple_of(8 * (i % 16), 8), 8)
        col = [prods[c, r, rows, :] for r in range(PROWS)]
        for x in range(16):
            s = G4[12] * col[x + 12]
            for t in range(1, RAD_S + 1):
                s = s + G4[12 + t] * (col[x + 12 + t] + col[x + 12 - t])
            sums[c, x, rows, :] = s
        return carry

    lax.fori_loop(0, 96, smooth_x, 0)

    def smooth_z(i, carry):
        c = i // 4
        x = 4 * (i % 4)
        a = sums[c, pl.ds(x, 2)].reshape(256, LANES)
        b = sums[c, pl.ds(x + 2, 2)].reshape(256, LANES)
        sh, sl = split(jnp.concatenate([a, b], axis=1))
        o = dot(bh_ref[...], sh) + dot(bh_ref[...], sl) + dot(bl_ref[...], sh)
        first = pl.multiple_of(16 * i, 8)
        out_ref[:, pl.ds(first, 8), :] = o[:, :LANES].reshape(NB, 8, LANES)
        out_ref[:, pl.ds(first + 8, 8), :] = o[:, LANES:].reshape(NB, 8, LANES)
        return carry

    lax.fori_loop(0, 24, smooth_z, 0)


def tensor(place, left, own, right):
    gh, gl = halves(y_gradient_matrix())
    wh, wl = halves(z_gradient_matrix())
    bh, bl = halves(z_smooth_matrix())
    vmem = pl.BlockSpec(memory_space=pltpu.VMEM)
    return pl.pallas_call(
        tensor_kernel,
        out_shape=jax.ShapeDtypeStruct((NB, 384, LANES), F32),
        in_specs=[pl.BlockSpec(memory_space=pltpu.SMEM)] + [vmem] * 9,
        out_specs=vmem,
        scratch_shapes=[
            pltpu.VMEM((3, NROW, 128, LANES), F32),
            pltpu.VMEM((6, PROWS, 128, LANES), F32),
            pltpu.VMEM((6, 16, 128, LANES), F32),
        ],
        compiler_params=pltpu.CompilerParams(vmem_limit_bytes=60 * 2**20),
        name="tensor",
    )(place, left, own, right, *(jnp.asarray(m) for m in (gh, gl, wh, wl, bh, bl)))


def smooth_y_kernel(in_ref, mh_ref, ml_ref, out_ref):
    lane = lax.broadcasted_iota(jnp.int32, (64, LANES), 1)
    zero = jnp.zeros((64, LANES), F32)
    for j in range(0, NB, 2):
        before = in_ref[j - 1] if j > 0 else zero
        after = in_ref[j + 2] if j + 2 < NB else zero
        rims = jnp.where(lane < 64, after, before)
        xh, xl = split(jnp.concatenate([in_ref[j], in_ref[j + 1], rims], axis=1))
        o = dot(xh, mh_ref[...]) + dot(xl, mh_ref[...]) + dot(xh, ml_ref[...])
        for x in range(16):
            out_ref[0, x, :, 128 * j : 128 * j + 256] = o[4 * x : 4 * x + 4, :]


def smooth_y(received):
    mh, ml = halves(y_smooth_matrix())
    whole = pl.BlockSpec((384, 256), lambda c: (0, 0))
    return pl.pallas_call(
        smooth_y_kernel,
        grid=(6,),
        out_shape=jax.ShapeDtypeStruct((6, 16, 4, NB * LANES), F32),
        in_specs=[pl.BlockSpec((NB, 64, LANES), lambda c: (0, c, 0)), whole, whole],
        out_specs=pl.BlockSpec((1, 16, 4, NB * LANES), lambda c: (c, 0, 0, 0)),
        compiler_params=pltpu.CompilerParams(vmem_limit_bytes=40 * 2**20),
        name="smooth_y",
    )(received, jnp.asarray(mh), jnp.asarray(ml))


def on_device(volume, occupancy):
    message = pack(volume, occupancy)
    columns = lax.all_to_all(message, "dev", 0, 0, tiled=True)
    size = lax.axis_size("gx")
    up = [(i, i + 1) for i in range(size - 1)]
    down = [(i + 1, i) for i in range(size - 1)]
    left = lax.ppermute(columns, "gx", up)
    right = lax.ppermute(columns, "gx", down)
    place = lax.axis_index("gx").reshape(1)
    blocks = tensor(place, left, columns, right)
    received = lax.all_to_all(blocks, "dev", 0, 0, tiled=True)
    return smooth_y(received)


def solution(mesh):
    return jax.shard_map(
        on_device,
        mesh=mesh,
        in_specs=(P("gx", "dev", None), P("gx", "dev")),
        out_specs=P(None, "gx", "dev", None),
        check_vma=False,
    )
```

time: 854 us -> 175 us (0.20); the launches traced: 840 us -> 175 us
  other arithmetic: 361 us -> 0 us
  local copies, waits for them, and re-layouts: 256 us -> 2.36 us
  Pallas kernels: 0 us -> 56.7 us
  blocking collectives: 147 us -> 94.5 us
  waiting for transfers between devices: 58.5 us -> 13.1 us
  starting transfers between devices: 17 us -> 8.22 us
    add x6 -> x0, other arithmetic: 319 us -> none  [line_pass(): summed + float(weights[offset]) * lax.slice_in_dim(source, offset, offset...]
    unnamed x7 -> x11, local copies, waits for them, and re-layouts: 127 us -> 2.36 us
    all_to_all x8 -> x0, local copies, waits for them, and re-layouts: 65 us -> none  [the longest x1 38.9 us: on_device(): lax.all_to_all(tensor, 'dev', split_axis=3, concat_axis=2, tiled=True)]
    pallas_call x0 -> x3, Pallas kernels: none -> 56.7 us  [the longest x1 41.9 us: tensor(): pl.pallas_call(tensor_kernel, out_shape=jax.ShapeDtypeStruct((NB, 384, LA...]
    all_to_all x4 -> x2, blocking collectives: 147 us -> 94.5 us  [the longest x1 66.5 us: on_device(): received = lax.all_to_all(blocks, 'dev', 0, 0, tiled=True)]
    ppermute x4 -> x2, waiting for transfers between devices: 58.5 us -> 13.1 us  [the longest x1 11.9 us: on_device(): right = lax.ppermute(columns, 'gx', down)]
    add x2 -> x0, local copies, waits for them, and re-layouts: 40.9 us -> none  [line_pass(): summed + float(weights[offset]) * lax.slice_in_dim(source, offset, offset...]
    all_to_all x2 -> x0, other arithmetic: 22.7 us -> none  [the longest x1 19.5 us: on_device(): lax.all_to_all(tensor, 'dev', split_axis=3, concat_axis=2, tiled=True)]
  transfers between devices with their start and end apart: 4 -> 2, of which waited for: 4 -> 2; matrix products, arithmetic and copies ran while one was open for 1% -> 0% of each run, Pallas kernels for 0% -> 0%
where the time goes in v1:
time: 175 us
  blocking collectives  94.5 us (54%)
  Pallas kernels  56.7 us (32%)
  waiting for transfers between devices  13.1 us (7%)
  starting transfers between devices  8.22 us (5%)
  local copies, waits for them, and re-layouts  2.36 us (1%)
    all_to_all x1, blocking collectives, on_device(): received = lax.all_to_all(blocks, 'dev', 0, 0, tiled=True)  66.5 us
    pallas_call x1, Pallas kernels, tensor(): pl.pallas_call(tensor_kernel, out_shape=jax.ShapeDtypeStruct((NB, 384, LA...  41.9 us
    all_to_all x1, blocking collectives, on_device(): columns = lax.all_to_all(message, 'dev', 0, 0, tiled=True)  28 us
    pallas_call x1, Pallas kernels, smooth_y(): pl.pallas_call(smooth_y_kernel, grid=(6,), out_shape=jax.ShapeDtypeStruct...  12.2 us
    ppermute x1, waiting for transfers between devices, on_device(): right = lax.ppermute(columns, 'gx', down)  11.9 us
    ppermute x1, starting transfers between devices, on_device(): left = lax.ppermute(columns, 'gx', up)  4.26 us
    ppermute x1, starting transfers between devices, on_device(): right = lax.ppermute(columns, 'gx', down)  3.96 us
  transfers between devices with their start and end apart: 2, of which 2 were waited for; matrix products, arithmetic and copies ran while one was open for 0% of the time, Pallas kernels for 0%

profile of v1, /device:TPU:1, one launch (start us, length us, event | category | flops | bytes accessed | tf_op | source)
XLA Modules:
  0.0 175.0 jit_solution(17133601258782090142)
XLA Ops:
  0.0 1.3 copy.11.occ_ref
  1.3 2.6 %pack.1 = f32[32,72,128]{2,1,0:T(8,128)} custom-call(s32[2,1]{1,0:T(2,128)} %copy.11.occ_ref, f32[16,4,4096]{2,1,0:T(4,128)} %vol_ref.1), custom_call_target="tpu_custom_call" | custom-call | tf_op jit(solution)/shard_map/pack/pallas_call | solution.py:133
  4.0 28.0 %all_to_all.10.own_ref = f32[32,72,128]{2,1,0:T(8,128)S(1)} all-to-all(f32[32,72,128]{2,1,0:T(8,128)} %pack.1), channel_id=1, replica_groups=mesh['gx'=4,'dev'=32] {'dev'}, dimensions={0} | all-to-all | bytes 2359296 | tf_op jit(solution)/shard_map/all_to_all | solution.py:288
  32.0 0.0 copy-start.2
  32.0 4.0 %collective-permute-start.1 = (f32[32,72,128]{2,1,0:T(8,128)S(1)}, f32[32,72,128]{2,1,0:T(8,128)S(1)}, u32[]{:S(2)}, u32[]{:S(2)}) collective-permute-start(f32[32,72,128]{2,1,0:T(8,128)S(1)} %all_to_all.10.own_ref), channel_id=1, source_target_pairs={{32,0},{64,32},{96,64},{33,1},{65,33},{97,65},{34,2},{66,34},{98,6... | collective-permute-start | bytes 3538952 | tf_op jit(solution)/shard_map/ppermute | solution.py:293
  35.9 4.3 %collective-permute-start = (f32[32,72,128]{2,1,0:T(8,128)S(1)}, f32[32,72,128]{2,1,0:T(8,128)S(1)}, u32[]{:S(2)}, u32[]{:S(2)}) collective-permute-start(f32[32,72,128]{2,1,0:T(8,128)S(1)} %all_to_all.10.own_ref), channel_id=1, source_target_pairs={{0,32},{32,64},{64,96},{1,33},{33,65},{65,97},{2,34},{34,66},{66,9... | collective-permute-start | bytes 3538952 | tf_op jit(solution)/shard_map/ppermute | solution.py:292
  40.2 11.9 %collective-permute-done.1.right_ref = f32[32,72,128]{2,1,0:T(8,128)S(1)} collective-permute-done((f32[32,72,128]{2,1,0:T(8,128)S(1)}, f32[32,72,128]{2,1,0:T(8,128)S(1)}, u32[]{:S(2)}, u32[]{:S(2)}) %collective-permute-start.1) | collective-permute-done | bytes 1179680 | tf_op jit(solution)/shard_map/ppermute | solution.py:293
  52.1 0.0 copy-start.3
  52.1 1.2 collective-permute-done.left_ref
  53.3 0.0 copy-start.4
  53.3 0.0 copy-done.2
  53.3 0.0 copy-done.3
  53.3 1.0 copy-done.4
  54.3 41.9 %tensor.1 = f32[32,384,128]{2,1,0:T(8,128)} custom-call(s32[1]{0:T(128)} %bitcast.edge_ref, f32[32,72,128]{2,1,0:T(8,128)} %copy-done.4, f32[32,72,128]{2,1,0:T(8,128)} %copy-done.2, f32[32,72,128]{2,1,0:T(8,128)} %copy-done.3, bf16[256,256]{1,0:T(8,128)(2,1)} %constant.22.clone.gh_ref, bf16[256,256]{1,0:T(8,128)(2,1)} %constant.23.clone.gl_ref, ...), custom_call_target="tpu_custom_call" | custom-call | tf_op jit(solution)/shard_map/tensor/pallas_call | solution.py:244
  96.3 0.0 copy-start
  96.3 0.0 copy-start.1
  96.3 66.5 %all_to_all.11.in_ref = f32[32,384,128]{2,1,0:T(8,128)S(1)} all-to-all(f32[32,384,128]{2,1,0:T(8,128)} %tensor.1), channel_id=1, replica_groups=mesh['gx'=4,'dev'=32] {'dev'}, dimensions={0} | all-to-all | bytes 12582912 | tf_op jit(solution)/shard_map/all_to_all | solution.py:296
  162.8 0.0 copy-done
  162.8 0.0 copy-done.1
  162.8 12.2 %smooth_y.1 = f32[6,16,4,4096]{3,2,1,0:T(4,128)} custom-call(f32[32,384,128]{2,1,0:T(8,128)S(1)} %all_to_all.11.in_ref, bf16[384,256]{1,0:T(8,128)(2,1)S(1)} %copy-done.1, bf16[384,256]{1,0:T(8,128)(2,1)S(1)} %copy-done), custom_call_target="tpu_custom_call" | custom-call | tf_op jit(solution)/shard_map/smooth_y/pallas_call | solution.py:275
Async XLA Ops:
  32.0 21.4 %copy-start.2 = (f32[32,72,128]{2,1,0:T(8,128)}, f32[32,72,128]{2,1,0:T(8,128)S(1)}, u32[]{:S(2)}) copy-start(f32[32,72,128]{2,1,0:T(8,128)S(1)} %all_to_all.10.own_ref) | copy-start | bytes 3538948
  32.0 20.2 %collective-permute-start.1 = (f32[32,72,128]{2,1,0:T(8,128)S(1)}, f32[32,72,128]{2,1,0:T(8,128)S(1)}, u32[]{:S(2)}, u32[]{:S(2)}) collective-permute-start(f32[32,72,128]{2,1,0:T(8,128)S(1)} %all_to_all.10.own_ref), channel_id=1, source_target_pairs={{32,0},{64,32},{96,64},{33,1},{65,33},{97,65},{34,2},{66,34},{98,6... | collective-permute-start | bytes 3538952 | tf_op jit(solution)/shard_map/ppermute | solution.py:293
  35.9 17.4 %collective-permute-start = (f32[32,72,128]{2,1,0:T(8,128)S(1)}, f32[32,72,128]{2,1,0:T(8,128)S(1)}, u32[]{:S(2)}, u32[]{:S(2)}) collective-permute-start(f32[32,72,128]{2,1,0:T(8,128)S(1)} %all_to_all.10.own_ref), channel_id=1, source_target_pairs={{0,32},{32,64},{64,96},{1,33},{33,65},{65,97},{2,34},{34,66},{66,9... | collective-permute-start | bytes 3538952 | tf_op jit(solution)/shard_map/ppermute | solution.py:292
  52.1 1.2 copy-start.3
  53.3 1.0 copy-start.4
  96.3 66.5 %copy-start = (bf16[384,256]{1,0:T(8,128)(2,1)S(1)}, bf16[384,256]{1,0:T(8,128)(2,1)}, u32[]{:S(2)}) copy-start(bf16[384,256]{1,0:T(8,128)(2,1)} %constant.29.clone.ml_ref) | copy-start | bytes 589828
  96.3 66.5 %copy-start.1 = (bf16[384,256]{1,0:T(8,128)(2,1)S(1)}, bf16[384,256]{1,0:T(8,128)(2,1)}, u32[]{:S(2)}) copy-start(bf16[384,256]{1,0:T(8,128)(2,1)} %constant.28.clone.mh_ref) | copy-start | bytes 589828

commit v2 on v1

v2 whole, which is shorter than its diff:
```python
import math

import jax
import jax.numpy as jnp
import ml_dtypes
import numpy as np
from jax import lax
from jax.experimental import pallas as pl
from jax.experimental.pallas import tpu as pltpu
from jax.sharding import PartitionSpec as P

RAD_D = 3
RAD_S = 12
SIGMA_DERIV = 1.0
SIGMA_SMOOTH = 4.0

NB = 32
LANES = 128
HALO_SLOT = 16
MSG_ROWS = 72
F32 = jnp.float32
BF16 = jnp.bfloat16


def kernel_taps(radius, width_sigma, derivative):
    offsets = [float(t) for t in range(-radius, radius + 1)]
    weights = [math.exp(-0.5 * (t / width_sigma) ** 2) for t in offsets]
    if derivative:
        total = sum((t * t * w for t, w in zip(offsets, weights)))
        return [t * w / total for t, w in zip(offsets, weights)]
    total = sum(weights)
    return [w / total for w in weights]


G1 = kernel_taps(RAD_D, SIGMA_DERIV, False)
D1 = kernel_taps(RAD_D, SIGMA_DERIV, True)
G4 = kernel_taps(RAD_S, SIGMA_SMOOTH, False)


def halves(matrix):
    high = matrix.astype(ml_dtypes.bfloat16)
    low = (matrix - high.astype(np.float64)).astype(ml_dtypes.bfloat16)
    return high, low


def band(taps, n):
    radius = len(taps) // 2
    m = np.zeros((n, n))
    for i in range(n):
        for t in range(-radius, radius + 1):
            if 0 <= i + t < n:
                m[i, i + t] = taps[t + radius]
    return m


def y_gradient_matrix():
    m = np.zeros((2 * LANES, 2 * LANES))
    for part, taps in enumerate((G1, D1)):
        for y in range(LANES):
            for t in range(-RAD_D, RAD_D + 1):
                s = y + t
                w = taps[t + RAD_D]
                col = part * LANES + y
                if 0 <= s < LANES:
                    m[s, col] = w
                else:
                    k = s + RAD_D if s < 0 else RAD_D + s - LANES
                    for seg in range(8):
                        m[LANES + seg * HALO_SLOT + k, col] = w
    return m


def pair_order():
    return [(xp, 4 * d + z) for d in range(NB) for xp in range(2) for z in range(4)]


def z_gradient_matrix():
    return np.concatenate([band(G1, 128), band(D1, 128)], axis=0)


def z_smooth_matrix():
    smooth = band(G4, 128)
    m = np.zeros((256, 256))
    for row, (xp, z) in enumerate(pair_order()):
        m[row, xp * 128 : xp * 128 + 128] = smooth[z]
    return m


def y_smooth_matrix():
    m = np.zeros((384, 256))
    for y in range(256):
        for t in range(-RAD_S, RAD_S + 1):
            s = y + t
            if s < 0:
                s = 256 + 128 + s
            elif s >= 256:
                s = 256 + s - 256
            m[s, y] = G4[t + RAD_S]
    return m


def split(x):
    high = x.astype(BF16)
    return high, (x - high.astype(F32)).astype(BF16)


def dot(a, b):
    return jnp.dot(a, b, preferred_element_type=F32)


def pack_kernel(occ_ref, vol_ref, out_ref):
    lane = lax.broadcasted_iota(jnp.int32, (8, LANES), 1)
    for p in range(8):
        present = occ_ref[0, p // 4].astype(F32)
        rows = jnp.concatenate([vol_ref[2 * p], vol_ref[2 * p + 1]], axis=0) * present
        blocks = [rows[:, j * LANES : (j + 1) * LANES] for j in range(NB)]
        zero = jnp.zeros((8, LANES), F32)
        for j in range(NB):
            out_ref[j, 8 * p : 8 * p + 8, :] = blocks[j]
            before = blocks[j - 1] if j > 0 else zero
            after = blocks[j + 1] if j < NB - 1 else zero
            rim = jnp.where(lane >= LANES - 3, before, jnp.where(lane < 3, after, 0.0))
            rim = pltpu.roll(rim, 3, 1, stride=HALO_SLOT, stride_axis=0)
            out_ref[j, 64 + p, :] = jnp.sum(rim, axis=0)


def pack(volume, occupancy):
    return pl.pallas_call(
        pack_kernel,
        out_shape=jax.ShapeDtypeStruct((NB, MSG_ROWS, LANES), F32),
        in_specs=[
            pl.BlockSpec(memory_space=pltpu.SMEM),
            pl.BlockSpec(memory_space=pltpu.VMEM),
        ],
        out_specs=pl.BlockSpec(memory_space=pltpu.VMEM),
        name="pack",
    )(occupancy.T, volume)


NROW = 48
PROWS = 40
BLOCKS_OUT = pltpu.VMEM
CHUNKS = ((0, 1, 2, 3, 4, 5),)


def smooth_products(chunk, grads, b_ref, out_ref, sums):
    def along_x(step):
        k = step // 4
        c = chunk[0] + k
        first = (c > 2).astype(jnp.int32) + (c > 4).astype(jnp.int32)
        second = c - 2 * (c > 2).astype(jnp.int32) - (c > 4).astype(jnp.int32)
        for q in range(4):
            rows = pl.ds(pl.multiple_of(32 * (step % 4) + 8 * q, 8), 8)
            col = [grads[first, r, rows, :] * grads[second, r, rows, :] for r in range(PROWS)]
            for x in range(16):
                s = G4[12] * col[x + 12]
                for t in range(1, RAD_S + 1):
                    s = s + G4[12 + t] * (col[x + 12 + t] + col[x + 12 - t])
                sums[k % 2, x, rows, :] = s

    def along_depth(step):
        k, x = step // 4, 4 * (step % 4)
        a = sums[k % 2, pl.ds(x, 2)].reshape(256, LANES)
        b = sums[k % 2, pl.ds(x + 2, 2)].reshape(256, LANES)
        sh, sl = split(jnp.concatenate([a, b], axis=1))
        o = dot(b_ref[...], jnp.concatenate([sh, sl, sh], axis=0))
        first = pl.multiple_of(16 * step, 16)
        out_ref[:, pl.ds(first, 8), :] = o[:, :LANES].reshape(NB, 8, LANES)
        out_ref[:, pl.ds(first + 8, 8), :] = o[:, LANES:].reshape(NB, 8, LANES)

    def end(step, carry):
        along_depth(step)
        return carry

    def begin(step, carry):
        along_x(step)
        return carry

    for k in range(len(chunk)):
        lax.fori_loop(4 * k, 4 * k + 4, begin, 0)
        lax.fori_loop(4 * k, 4 * k + 4, end, 0, unroll=4)


def gradient_kernel(
    place_ref, own_ref, partner_ref, cross_ref, g_ref, w_ref, b_ref, out_ref, *refs
):
    if len(CHUNKS) > 1:
        kept_ref, fields, grads, sums, sem = refs
    else:
        fields, grads, sums = refs
    place = place_ref[0]
    odd = place % 2
    row = lax.broadcasted_iota(jnp.int32, (8, LANES), 0)
    lane = lax.broadcasted_iota(jnp.int32, (8, LANES), 1)
    mine = (row == lane // HALO_SLOT)[None]

    bases = (16, 32 - 32 * odd, 32 * odd)
    for base, src in zip(bases, (own_ref, partner_ref, cross_ref)):

        def pair(p, carry, base=base, src=src):
            first = pl.multiple_of(8 * p, 8)
            main = src[:, pl.ds(first, 8), :]
            rim = src[:, pl.ds(64 + p, 1), :]
            rim = jnp.where(mine, jnp.broadcast_to(rim, (NB, 8, LANES)), 0.0)
            rows = [main[:, :4].reshape(128, LANES), main[:, 4:].reshape(128, LANES)]
            rims = [rim[:, :4].reshape(128, LANES), rim[:, 4:].reshape(128, LANES)]
            both = jnp.concatenate(
                [jnp.concatenate(rows, axis=0), jnp.concatenate(rims, axis=0)], axis=1
            )
            xh, xl = split(both)
            y = dot(jnp.concatenate([xh, xl, xh], axis=1), g_ref[...])
            yh, yl = split(y)

            def lanes(m, k):
                k = k * LANES
                return jnp.concatenate([m[:128, k : k + LANES], m[128:, k : k + LANES]], axis=1)

            sh, sl = lanes(yh, 0), lanes(yl, 0)
            dh, dl = lanes(yh, 1), lanes(yl, 1)
            both = dot(w_ref[...], jnp.concatenate([sh, sl, sh], axis=0))
            other = dot(w_ref[:128, :], jnp.concatenate([dh, dl, dh], axis=0))
            e = base + 2 * p
            for k in range(2):
                cols = slice(k * LANES, (k + 1) * LANES)
                fields[0, e + k] = both[:128, cols]
                fields[1, e + k] = other[:, cols]
                fields[2, e + k] = both[128:, cols]
            return carry

        lax.fori_loop(0, 8, pair, 0, unroll=8)

    def gradient_row(r, carry):
        keep = jnp.where((r < 12) & (place == 0), 0.0, 1.0)
        keep = jnp.where((r >= 28) & (place == 3), 0.0, keep)
        for zt in range(16):
            rows = pl.ds(8 * zt, 8)

            def tap(f, t):
                return fields[f, r + (4 + t), rows, :]

            def sym(f):
                s = G1[3] * tap(f, 0)
                for t in (1, 2, 3):
                    s = s + G1[3 + t] * (tap(f, t) + tap(f, -t))
                return s * keep

            gx = D1[4] * (tap(0, 1) - tap(0, -1))
            for t in (2, 3):
                gx = gx + D1[3 + t] * (tap(0, t) - tap(0, -t))
            grads[0, r, rows, :] = gx * keep
            grads[1, r, rows, :] = sym(1)
            grads[2, r, rows, :] = sym(2)
        return carry

    lax.fori_loop(0, PROWS, gradient_row, 0, unroll=2)

    if len(CHUNKS) > 1:
        keep = pltpu.make_async_copy(grads, kept_ref, sem)
        keep.start()
    smooth_products(CHUNKS[0], grads, b_ref, out_ref, sums)
    if len(CHUNKS) > 1:
        keep.wait()


def product_kernel(chunk, grads, b_ref, out_ref, sums):
    smooth_products(chunk, grads, b_ref, out_ref, sums)


VMEM = pl.BlockSpec(memory_space=pltpu.VMEM)
FIELDS = (3, PROWS, 128, LANES)
SUMS = pltpu.VMEM((2, 16, 128, LANES), F32)


def gradients(place, own, partner, cross):
    gh, gl = halves(y_gradient_matrix())
    wh, wl = halves(z_gradient_matrix())
    g = np.concatenate([gh, gh, gl], axis=0)
    w = np.concatenate([wh, wh, wl], axis=1)
    blocks = (NB, 64 * len(CHUNKS[0]), LANES)
    scratch = [pltpu.VMEM((3, NROW, 128, LANES), F32), pltpu.VMEM(FIELDS, F32), SUMS]
    if len(CHUNKS) > 1:
        out_shape = (pltpu.HBM(blocks, F32), pltpu.HBM(FIELDS, F32))
        out_specs = (VMEM, pl.BlockSpec(memory_space=pl.ANY))
        scratch.append(pltpu.SemaphoreType.DMA)
    else:
        out_shape, out_specs = (BLOCKS_OUT(blocks, F32),), (VMEM,)
    return pl.pallas_call(
        gradient_kernel,
        out_shape=out_shape,
        in_specs=[pl.BlockSpec(memory_space=pltpu.SMEM)] + [VMEM] * 6,
        out_specs=out_specs,
        scratch_shapes=scratch,
        compiler_params=pltpu.CompilerParams(vmem_limit_bytes=36 * 2**20),
        cost_estimate=pl.CostEstimate(flops=10**10, transcendentals=0, bytes_accessed=2 * 10**7),
        name="gradients",
    )(place, own, partner, cross, in_hbm(g), in_hbm(w), smooth_matrix())


def in_hbm(m):
    return pltpu.with_memory_space_constraint(jnp.asarray(m), pltpu.HBM)


def smooth_matrix():
    bh, bl = halves(z_smooth_matrix())
    return in_hbm(np.concatenate([bh, bh, bl], axis=1))


def smoothed_products(grads, chunk):
    return pl.pallas_call(
        lambda *refs: product_kernel(chunk, *refs),
        out_shape=pltpu.HBM((NB, 64 * len(chunk), LANES), F32),
        in_specs=[VMEM, VMEM],
        out_specs=VMEM,
        scratch_shapes=[SUMS],
        compiler_params=pltpu.CompilerParams(vmem_limit_bytes=24 * 2**20),
        cost_estimate=pl.CostEstimate(flops=10**10, transcendentals=0, bytes_accessed=2 * 10**7),
        name="products",
    )(grads, smooth_matrix())


GROUP = 8


def smooth_y_kernel(in_ref, m_ref, *refs):
    out_ref = refs[-1]
    lane = lax.broadcasted_iota(jnp.int32, (64, LANES), 1)
    zero = jnp.zeros((64, LANES), F32)
    for start in range(0, NB, 2 * GROUP):
        stack = []
        for j in range(start, start + 2 * GROUP, 2):
            before = in_ref[j - 1] if j > 0 else zero
            after = in_ref[j + 2] if j + 2 < NB else zero
            rims = jnp.where(lane < 64, after, before)
            xh, xl = split(jnp.concatenate([in_ref[j], in_ref[j + 1], rims], axis=1))
            stack.append(jnp.concatenate([xh, xl, xh], axis=1))
        o = dot(jnp.concatenate(stack, axis=0), m_ref[...])
        for k in range(GROUP):
            j = start + 2 * k
            for x in range(16):
                first = 64 * k + 4 * x
                out_ref[0, x, :, 128 * j : 128 * j + 256] = o[first : first + 4, :]


def smooth_y(received, where, out):
    mh, ml = halves(y_smooth_matrix())
    m = in_hbm(np.concatenate([mh, mh, ml], axis=0))
    first = where[0]
    args = [received, m] + ([] if out is None else [out])
    return pl.pallas_call(
        smooth_y_kernel,
        grid=(len(where),),
        out_shape=jax.ShapeDtypeStruct((6, 16, 4, NB * LANES), F32),
        in_specs=[pl.BlockSpec((NB, 64, LANES), lambda c: (0, c, 0)), VMEM]
        + [pl.BlockSpec(memory_space=pl.ANY)] * (len(args) - 2),
        out_specs=pl.BlockSpec((1, 16, 4, NB * LANES), lambda c: (first + c, 0, 0, 0)),
        input_output_aliases={} if out is None else {2: 0},
        compiler_params=pltpu.CompilerParams(vmem_limit_bytes=24 * 2**20),
        cost_estimate=pl.CostEstimate(flops=6 * 10**9, transcendentals=0, bytes_accessed=10**7),
        name="smooth_y",
    )(*args)


def on_device(volume, occupancy):
    message = pack(volume, occupancy)
    columns = lax.all_to_all(message, "dev", 0, 0, tiled=True)
    partner = lax.ppermute(columns, "gx", [(0, 1), (1, 0), (2, 3), (3, 2)])
    cross = lax.ppermute(columns, "gx", [(1, 2), (2, 1)])
    place = lax.axis_index("gx").reshape(1)
    blocks, *grads = gradients(place, columns, partner, cross)
    received = [lax.all_to_all(blocks, "dev", 0, 0, tiled=True)]
    for chunk in CHUNKS[1:]:
        blocks = smoothed_products(grads[0], chunk)
        received.append(lax.all_to_all(blocks, "dev", 0, 0, tiled=True))
    out = None
    for chunk, part in zip(CHUNKS, received):
        out = smooth_y(part, chunk, out)
    return out


def solution(mesh):
    return jax.shard_map(
        on_device,
        mesh=mesh,
        in_specs=(P("gx", "dev", None), P("gx", "dev")),
        out_specs=P(None, "gx", "dev", None),
        check_vma=False,
    )
```

time: 175 us -> 149 us (0.85)
  Pallas kernels: 56.7 us -> 32.9 us
  local copies, waits for them, and re-layouts: 2.36 us -> 0 us
  starting transfers between devices: 8.22 us -> 6.38 us
    pallas_call x2, Pallas kernels: 54.1 us -> 30.2 us  [the longest x1 22.5 us: gradients(): pl.pallas_call(gradient_kernel, out_shape=out_shape, in_specs=[pl.BlockSp...]
    unnamed x11 -> x0, local copies, waits for them, and re-layouts: 2.36 us -> none
    ppermute x2, starting transfers between devices: 8.22 us -> 6.38 us  [the longest x1 6.3 us: on_device(): cross = lax.ppermute(columns, 'gx', [(1, 2), (2, 1)])]
  transfers between devices with their start and end apart: 2 -> 2, of which waited for: 2 -> 1; matrix products, arithmetic and copies ran while one was open for 0% -> 0% of each run, Pallas kernels for 0% -> 0%
where the time goes in v2:
time: 149 us
  blocking collectives  95.5 us (64%)
  Pallas kernels  32.9 us (22%)
  waiting for transfers between devices  13.8 us (9%)
  starting transfers between devices  6.38 us (4%)
    all_to_all x1, blocking collectives, on_device(): received = [lax.all_to_all(blocks, 'dev', 0, 0, tiled=True)]  67.5 us
    all_to_all x1, blocking collectives, on_device(): columns = lax.all_to_all(message, 'dev', 0, 0, tiled=True)  28 us
    pallas_call x1, Pallas kernels, gradients(): pl.pallas_call(gradient_kernel, out_shape=out_shape, in_specs=[pl.BlockSp...  22.5 us
    ppermute x1, waiting for transfers between devices, on_device(): cross = lax.ppermute(columns, 'gx', [(1, 2), (2, 1)])  13.8 us
    pallas_call x1, Pallas kernels, smooth_y(): pl.pallas_call(smooth_y_kernel, grid=(len(where),), out_shape=jax.ShapeDt...  7.67 us
    ppermute x1, starting transfers between devices, on_device(): cross = lax.ppermute(columns, 'gx', [(1, 2), (2, 1)])  6.3 us
  transfers between devices with their start and end apart: 2, of which 1 were waited for; matrix products, arithmetic and copies ran while one was open for 0% of the time, Pallas kernels for 0%

profile of v2, /device:TPU:1, one launch (start us, length us, event | category | flops | bytes accessed | tf_op | source)
XLA Modules:
  0.0 148.6 jit_solution(7212872434726573323)
XLA Ops:
  0.0 2.6 %pack.1 = f32[32,72,128]{2,1,0:T(8,128)} custom-call(s32[1,2]{1,0:T(1,128)} %bitcast.2, f32[16,4,4096]{2,1,0:T(4,128)} %vol_ref.1), custom_call_target="tpu_custom_call" | custom-call | tf_op jit(solution)/shard_map/pack/pallas_call | solution.py:128
  2.6 28.0 %all_to_all.10.own_ref = f32[32,72,128]{2,1,0:T(8,128)S(1)} all-to-all(f32[32,72,128]{2,1,0:T(8,128)} %pack.1), channel_id=1, replica_groups=mesh['gx'=4,'dev'=32] {'dev'}, dimensions={0} | all-to-all | bytes 2359296 | tf_op jit(solution)/shard_map/all_to_all | solution.py:365
  30.6 6.3 %collective-permute-start.1 = (f32[32,72,128]{2,1,0:T(8,128)S(1)}, f32[32,72,128]{2,1,0:T(8,128)S(1)}, u32[]{:S(2)}, u32[]{:S(2)}) collective-permute-start(f32[32,72,128]{2,1,0:T(8,128)S(1)} %all_to_all.10.own_ref), channel_id=1, source_target_pairs={{32,64},{64,32},{33,65},{65,33},{34,66},{66,34},{35,67},{67,35},{3... | collective-permute-start | bytes 3538952 | tf_op jit(solution)/shard_map/ppermute | solution.py:367
  36.9 0.1 collective-permute-start
  37.0 13.8 %collective-permute-done.1.cross_ref = f32[32,72,128]{2,1,0:T(8,128)S(1)} collective-permute-done((f32[32,72,128]{2,1,0:T(8,128)S(1)}, f32[32,72,128]{2,1,0:T(8,128)S(1)}, u32[]{:S(2)}, u32[]{:S(2)}) %collective-permute-start.1) | collective-permute-done | bytes 1179680 | tf_op jit(solution)/shard_map/ppermute | solution.py:367
  50.8 0.0 collective-permute-done.partner_ref
  50.8 22.5 %gradients.1 = f32[32,384,128]{2,1,0:T(8,128)S(1)} custom-call(s32[1]{0:T(128)} %bitcast.place_ref, f32[32,72,128]{2,1,0:T(8,128)S(1)} %all_to_all.10.own_ref, f32[32,72,128]{2,1,0:T(8,128)S(1)} %collective-permute-done.partner_ref, f32[32,72,128]{2,1,0:T(8,128)S(1)} %collective-permute-done.1.cross_ref, bf16[768,256]{1,0:T(8,128)(2,1)} %constant.14.clone.g_ref, ...), custom_call_target="tpu_custom_call" | custom-call | flops 10000000000 | bytes 20000000 | tf_op jit(solution)/shard_map/gradients/pallas_call | solution.py:287
  73.4 67.5 %all_to_all.11.in_ref = f32[32,384,128]{2,1,0:T(8,128)S(1)} all-to-all(f32[32,384,128]{2,1,0:T(8,128)S(1)} %gradients.1), channel_id=1, replica_groups=mesh['gx'=4,'dev'=32] {'dev'}, dimensions={0} | all-to-all | bytes 12582912 | tf_op jit(solution)/shard_map/all_to_all | solution.py:370
  140.9 7.7 %smooth_y.1 = f32[6,16,4,4096]{3,2,1,0:T(4,128)} custom-call(f32[32,384,128]{2,1,0:T(8,128)S(1)} %all_to_all.11.in_ref, bf16[1152,256]{1,0:T(8,128)(2,1)} %constant.17.clone.m_ref), custom_call_target="tpu_custom_call" | custom-call | flops 6000000000 | bytes 10000000 | tf_op jit(solution)/shard_map/smooth_y/pallas_call | solution.py:349
Async XLA Ops:
  30.6 20.2 %collective-permute-start.1 = (f32[32,72,128]{2,1,0:T(8,128)S(1)}, f32[32,72,128]{2,1,0:T(8,128)S(1)}, u32[]{:S(2)}, u32[]{:S(2)}) collective-permute-start(f32[32,72,128]{2,1,0:T(8,128)S(1)} %all_to_all.10.own_ref), channel_id=1, source_target_pairs={{32,64},{64,32},{33,65},{65,33},{34,66},{66,34},{35,67},{67,35},{3... | collective-permute-start | bytes 3538952 | tf_op jit(solution)/shard_map/ppermute | solution.py:367
  36.9 13.9 %collective-permute-start = (f32[32,72,128]{2,1,0:T(8,128)S(1)}, f32[32,72,128]{2,1,0:T(8,128)S(1)}, u32[]{:S(2)}, u32[]{:S(2)}) collective-permute-start(f32[32,72,128]{2,1,0:T(8,128)S(1)} %all_to_all.10.own_ref), channel_id=1, source_target_pairs={{0,32},{32,0},{64,96},{96,64},{1,33},{33,1},{65,97},{97,65},{2,34}... | collective-permute-start | bytes 3538952 | tf_op jit(solution)/shard_map/ppermute | solution.py:366

commit v3 on v2

--- a/solution.py
+++ b/solution.py
@@ -127,7 +127,7 @@
 def pack(volume, occupancy):
     return pl.pallas_call(
         pack_kernel,
-        out_shape=jax.ShapeDtypeStruct((NB, MSG_ROWS, LANES), F32),
+        out_shape=pltpu.VMEM((NB, MSG_ROWS, LANES), F32),
         in_specs=[
             pl.BlockSpec(memory_space=pltpu.SMEM),
             pl.BlockSpec(memory_space=pltpu.VMEM),
@@ -139,8 +139,6 @@
 
 NROW = 48
 PROWS = 40
-BLOCKS_OUT = pltpu.VMEM
-CHUNKS = ((0, 1, 2, 3, 4, 5),)
 
 
 def smooth_products(chunk, grads, b_ref, out_ref, sums):
@@ -181,55 +179,52 @@
         lax.fori_loop(4 * k, 4 * k + 4, end, 0, unroll=4)
 
 
-def gradient_kernel(
-    place_ref, own_ref, partner_ref, cross_ref, g_ref, w_ref, b_ref, out_ref, *refs
-):
-    if len(CHUNKS) > 1:
-        kept_ref, fields, grads, sums, sem = refs
-    else:
-        fields, grads, sums = refs
-    place = place_ref[0]
-    odd = place % 2
+NEAR = 25
+FAR = PROWS - NEAR
+EDGE = 6
+
+
+def line_fields(src, base, g_ref, w_ref, fields):
     row = lax.broadcasted_iota(jnp.int32, (8, LANES), 0)
     lane = lax.broadcasted_iota(jnp.int32, (8, LANES), 1)
     mine = (row == lane // HALO_SLOT)[None]
 
-    bases = (16, 32 - 32 * odd, 32 * odd)
-    for base, src in zip(bases, (own_ref, partner_ref, cross_ref)):
-
-        def pair(p, carry, base=base, src=src):
-            first = pl.multiple_of(8 * p, 8)
-            main = src[:, pl.ds(first, 8), :]
-            rim = src[:, pl.ds(64 + p, 1), :]
-            rim = jnp.where(mine, jnp.broadcast_to(rim, (NB, 8, LANES)), 0.0)
-            rows = [main[:, :4].reshape(128, LANES), main[:, 4:].reshape(128, LANES)]
-            rims = [rim[:, :4].reshape(128, LANES), rim[:, 4:].reshape(128, LANES)]
-            both = jnp.concatenate(
-                [jnp.concatenate(rows, axis=0), jnp.concatenate(rims, axis=0)], axis=1
-            )
-            xh, xl = split(both)
-            y = dot(jnp.concatenate([xh, xl, xh], axis=1), g_ref[...])
-            yh, yl = split(y)
-
-            def lanes(m, k):
-                k = k * LANES
-                return jnp.concatenate([m[:128, k : k + LANES], m[128:, k : k + LANES]], axis=1)
-
-            sh, sl = lanes(yh, 0), lanes(yl, 0)
-            dh, dl = lanes(yh, 1), lanes(yl, 1)
-            both = dot(w_ref[...], jnp.concatenate([sh, sl, sh], axis=0))
-            other = dot(w_ref[:128, :], jnp.concatenate([dh, dl, dh], axis=0))
-            e = base + 2 * p
-            for k in range(2):
-                cols = slice(k * LANES, (k + 1) * LANES)
-                fields[0, e + k] = both[:128, cols]
-                fields[1, e + k] = other[:, cols]
-                fields[2, e + k] = both[128:, cols]
-            return carry
-
-        lax.fori_loop(0, 8, pair, 0, unroll=8)
-
-    def gradient_row(r, carry):
+    def pair(p, carry):
+        first = pl.multiple_of(8 * p, 8)
+        main = src[:, pl.ds(first, 8), :]
+        rim = src[:, pl.ds(64 + p, 1), :]
+        rim = jnp.where(mine, jnp.broadcast_to(rim, (NB, 8, LANES)), 0.0)
+        rows = [main[:, :4].reshape(128, LANES), main[:, 4:].reshape(128, LANES)]
+        rims = [rim[:, :4].reshape(128, LANES), rim[:, 4:].reshape(128, LANES)]
+        both = jnp.concatenate(
+            [jnp.concatenate(rows, axis=0), jnp.concatenate(rims, axis=0)], axis=1
+        )
+        xh, xl = split(both)
+        y = dot(jnp.concatenate([xh, xl, xh], axis=1), g_ref[...])
+        yh, yl = split(y)
+
+        def lanes(m, k):
+            k = k * LANES
+            return jnp.concatenate([m[:128, k : k + LANES], m[128:, k : k + LANES]], axis=1)
+
+        sh, sl = lanes(yh, 0), lanes(yl, 0)
+        dh, dl = lanes(yh, 1), lanes(yl, 1)
+        both = dot(w_ref[...], jnp.concatenate([sh, sl, sh], axis=0))
+        other = dot(w_ref[:128, :], jnp.concatenate([dh, dl, dh], axis=0))
+        e = base + 2 * p
+        for k in range(2):
+            cols = slice(k * LANES, (k + 1) * LANES)
+            fields[0, e + k] = both[:128, cols]
+            fields[1, e + k] = other[:, cols]
+            fields[2, e + k] = both[128:, cols]
+        return carry
+
+    lax.fori_loop(0, 8, pair, 0, unroll=8)
+
+
+def gradient_rows(place, fields, start, count, out, out_start, unroll):
+    def one(i, carry):
+        r = start + i
         keep = jnp.where((r < 12) & (place == 0), 0.0, 1.0)
         keep = jnp.where((r >= 28) & (place == 3), 0.0, keep)
         for zt in range(16):
@@ -247,53 +242,90 @@
             gx = D1[4] * (tap(0, 1) - tap(0, -1))
             for t in (2, 3):
                 gx = gx + D1[3 + t] * (tap(0, t) - tap(0, -t))
-            grads[0, r, rows, :] = gx * keep
-            grads[1, r, rows, :] = sym(1)
-            grads[2, r, rows, :] = sym(2)
-        return carry
-
-    lax.fori_loop(0, PROWS, gradient_row, 0, unroll=2)
-
-    if len(CHUNKS) > 1:
-        keep = pltpu.make_async_copy(grads, kept_ref, sem)
-        keep.start()
-    smooth_products(CHUNKS[0], grads, b_ref, out_ref, sums)
-    if len(CHUNKS) > 1:
-        keep.wait()
-
-
-def product_kernel(chunk, grads, b_ref, out_ref, sums):
-    smooth_products(chunk, grads, b_ref, out_ref, sums)
+            out[0, out_start + i, rows, :] = gx * keep
+            out[1, out_start + i, rows, :] = sym(1)
+            out[2, out_start + i, rows, :] = sym(2)
+        return carry
+
+    lax.fori_loop(0, count, one, 0, unroll=unroll)
+
+
+def near_kernel(place_ref, own_ref, partner_ref, g_ref, w_ref, edge_ref, near_ref, fields):
+    place = place_ref[0]
+    odd = place % 2
+    line_fields(own_ref, 16, g_ref, w_ref, fields)
+    line_fields(partner_ref, 32 - 32 * odd, g_ref, w_ref, fields)
+    for f in range(3):
+        for k in range(EDGE):
+            edge_ref[f, k] = fields[f, 16 + 10 * odd + k]
+    gradient_rows(place, fields, FAR - FAR * odd, NEAR, near_ref, 0, 5)
+
+
+def far_kernel(
+    place_ref, cross_ref, edge_ref, near_ref, g_ref, w_ref, b_ref, out_ref, fields, grads, sums
+):
+    place = place_ref[0]
+    odd = place % 2
+    line_fields(cross_ref, 32 * odd, g_ref, w_ref, fields)
+    for f in range(3):
+        for k in range(EDGE):
+            fields[f, 16 + 10 * odd + k] = edge_ref[f, k]
+    far = NEAR * odd
+    gradient_rows(place, fields, far, FAR, grads, far, 3)
+
+    def copy(i, carry):
+        for f in range(3):
+            grads[f, FAR - FAR * odd + i] = near_ref[f, i]
+        return carry
+
+    lax.fori_loop(0, NEAR, copy, 0)
+    smooth_products(range(6), grads, b_ref, out_ref, sums)
 
 
 VMEM = pl.BlockSpec(memory_space=pltpu.VMEM)
-FIELDS = (3, PROWS, 128, LANES)
-SUMS = pltpu.VMEM((2, 16, 128, LANES), F32)
-
-
-def gradients(place, own, partner, cross):
+SMEM = pl.BlockSpec(memory_space=pltpu.SMEM)
+FIELDS = pltpu.VMEM((3, NROW, 128, LANES), F32)
+
+
+def gradient_matrices():
     gh, gl = halves(y_gradient_matrix())
     wh, wl = halves(z_gradient_matrix())
     g = np.concatenate([gh, gh, gl], axis=0)
     w = np.concatenate([wh, wh, wl], axis=1)
-    blocks = (NB, 64 * len(CHUNKS[0]), LANES)
-    scratch = [pltpu.VMEM((3, NROW, 128, LANES), F32), pltpu.VMEM(FIELDS, F32), SUMS]
-    if len(CHUNKS) > 1:
-        out_shape = (pltpu.HBM(blocks, F32), pltpu.HBM(FIELDS, F32))
-        out_specs = (VMEM, pl.BlockSpec(memory_space=pl.ANY))
-        scratch.append(pltpu.SemaphoreType.DMA)
-    else:
-        out_shape, out_specs = (BLOCKS_OUT(blocks, F32),), (VMEM,)
+    return in_hbm(g), in_hbm(w)
+
+
+def near_gradients(place, own, partner):
     return pl.pallas_call(
-        gradient_kernel,
-        out_shape=out_shape,
-        in_specs=[pl.BlockSpec(memory_space=pltpu.SMEM)] + [VMEM] * 6,
-        out_specs=out_specs,
-        scratch_shapes=scratch,
-        compiler_params=pltpu.CompilerParams(vmem_limit_bytes=36 * 2**20),
+        near_kernel,
+        out_shape=(
+            pltpu.VMEM((3, EDGE, 128, LANES), F32),
+            pltpu.VMEM((3, NEAR, 128, LANES), F32),
+        ),
+        in_specs=[SMEM] + [VMEM] * 4,
+        out_specs=(VMEM, VMEM),
+        scratch_shapes=[FIELDS],
+        compiler_params=pltpu.CompilerParams(vmem_limit_bytes=30 * 2**20),
         cost_estimate=pl.CostEstimate(flops=10**10, transcendentals=0, bytes_accessed=2 * 10**7),
-        name="gradients",
-    )(place, own, partner, cross, in_hbm(g), in_hbm(w), smooth_matrix())
+        name="near",
+    )(place, own, partner, *gradient_matrices())
+
+
+def products(place, cross, edge, near):
+    return pl.pallas_call(
+        far_kernel,
+        out_shape=pltpu.VMEM((NB, 384, LANES), F32),
+        in_specs=[SMEM] + [VMEM] * 6,
+        out_specs=VMEM,
+        scratch_shapes=[
+            FIELDS,
+            pltpu.VMEM((3, PROWS, 128, LANES), F32),
+            pltpu.VMEM((2, 16, 128, LANES), F32),
+        ],
+        compiler_params=pltpu.CompilerParams(vmem_limit_bytes=38 * 2**20),
+        cost_estimate=pl.CostEstimate(flops=10**10, transcendentals=0, bytes_accessed=2 * 10**7),
+        name="products",
+    )(place, cross, edge, near, *gradient_matrices(), smooth_matrix())
 
 
 def in_hbm(m):
@@ -305,24 +337,10 @@
     return in_hbm(np.concatenate([bh, bh, bl], axis=1))
 
 
-def smoothed_products(grads, chunk):
-    return pl.pallas_call(
-        lambda *refs: product_kernel(chunk, *refs),
-        out_shape=pltpu.HBM((NB, 64 * len(chunk), LANES), F32),
-        in_specs=[VMEM, VMEM],
-        out_specs=VMEM,
-        scratch_shapes=[SUMS],
-        compiler_params=pltpu.CompilerParams(vmem_limit_bytes=24 * 2**20),
-        cost_estimate=pl.CostEstimate(flops=10**10, transcendentals=0, bytes_accessed=2 * 10**7),
-        name="products",
-    )(grads, smooth_matrix())
-
-
 GROUP = 8
 
 
-def smooth_y_kernel(in_ref, m_ref, *refs):
-    out_ref = refs[-1]
+def smooth_y_kernel(in_ref, m_ref, out_ref):
     lane = lax.broadcasted_iota(jnp.int32, (64, LANES), 1)
     zero = jnp.zeros((64, LANES), F32)
     for start in range(0, NB, 2 * GROUP):
@@ -341,23 +359,19 @@
                 out_ref[0, x, :, 128 * j : 128 * j + 256] = o[first : first + 4, :]
 
 
-def smooth_y(received, where, out):
+def smooth_y(received):
     mh, ml = halves(y_smooth_matrix())
     m = in_hbm(np.concatenate([mh, mh, ml], axis=0))
-    first = where[0]
-    args = [received, m] + ([] if out is None else [out])
     return pl.pallas_call(
         smooth_y_kernel,
-        grid=(len(where),),
+        grid=(6,),
         out_shape=jax.ShapeDtypeStruct((6, 16, 4, NB * LANES), F32),
-        in_specs=[pl.BlockSpec((NB, 64, LANES), lambda c: (0, c, 0)), VMEM]
-        + [pl.BlockSpec(memory_space=pl.ANY)] * (len(args) - 2),
-        out_specs=pl.BlockSpec((1, 16, 4, NB * LANES), lambda c: (first + c, 0, 0, 0)),
-        input_output_aliases={} if out is None else {2: 0},
+        in_specs=[pl.BlockSpec((NB, 64, LANES), lambda c: (0, c, 0)), VMEM],
+        out_specs=pl.BlockSpec((1, 16, 4, NB * LANES), lambda c: (c, 0, 0, 0)),
         compiler_params=pltpu.CompilerParams(vmem_limit_bytes=24 * 2**20),
         cost_estimate=pl.CostEstimate(flops=6 * 10**9, transcendentals=0, bytes_accessed=10**7),
         name="smooth_y",
-    )(*args)
+    )(received, m)
 
 
 def on_device(volume, occupancy):
@@ -366,15 +380,10 @@
     partner = lax.ppermute(columns, "gx", [(0, 1), (1, 0), (2, 3), (3, 2)])
     cross = lax.ppermute(columns, "gx", [(1, 2), (2, 1)])
     place = lax.axis_index("gx").reshape(1)
-    blocks, *grads = gradients(place, columns, partner, cross)
-    received = [lax.all_to_all(blocks, "dev", 0, 0, tiled=True)]
-    for chunk in CHUNKS[1:]:
-        blocks = smoothed_products(grads[0], chunk)
-        received.append(lax.all_to_all(blocks, "dev", 0, 0, tiled=True))
-    out = None
-    for chunk, part in zip(CHUNKS, received):
-        out = smooth_y(part, chunk, out)
-    return out
+    edge, near = near_gradients(place, columns, partner)
+    blocks = products(place, cross, edge, near)
+    received = lax.all_to_all(blocks, "dev", 0, 0, tiled=True)
+    return smooth_y(received)
 
 
 def solution(mesh):

time: 149 us -> 145 us (0.973)
  waiting for transfers between devices: 13.8 us -> 8.01 us
    ppermute x1, waiting for transfers between devices: 13.8 us -> 8.01 us  [on_device(): cross = lax.ppermute(columns, 'gx', [(1, 2), (2, 1)])]
    ppermute x1, starting transfers between devices: 6.3 us -> 4.24 us  [on_device(): cross = lax.ppermute(columns, 'gx', [(1, 2), (2, 1)])]
    ppermute x1, starting transfers between devices: 0.09 us -> 2.06 us  [on_device(): partner = lax.ppermute(columns, 'gx', [(0, 1), (1, 0), (2, 3), (3, 2)])]
    pallas_call x3 -> x4, Pallas kernels: 32.9 us -> 33.8 us  [the longest x1 17.8 us: products(): pl.pallas_call(far_kernel, out_shape=pltpu.VMEM((NB, 384, LANES), F32), i...]
  transfers between devices with their start and end apart: 2 -> 2, of which waited for: 1 -> 1; matrix products, arithmetic and copies ran while one was open for 0% -> 0% of each run, Pallas kernels for 0% -> 5%
where the time goes in v3:
time: 145 us
  blocking collectives  96.7 us (67%)
  Pallas kernels  33.8 us (23%)
  waiting for transfers between devices  8.01 us (6%)
  starting transfers between devices  6.3 us (4%)
    all_to_all x1, blocking collectives, on_device(): received = lax.all_to_all(blocks, 'dev', 0, 0, tiled=True)  68.9 us
    all_to_all x1, blocking collectives, on_device(): columns = lax.all_to_all(message, 'dev', 0, 0, tiled=True)  27.8 us
    pallas_call x1, Pallas kernels, products(): pl.pallas_call(far_kernel, out_shape=pltpu.VMEM((NB, 384, LANES), F32), i...  17.8 us
    ppermute x1, waiting for transfers between devices, on_device(): cross = lax.ppermute(columns, 'gx', [(1, 2), (2, 1)])  8.01 us
    pallas_call x1, Pallas kernels, smooth_y(): pl.pallas_call(smooth_y_kernel, grid=(6,), out_shape=jax.ShapeDtypeStruct...  7.67 us
    pallas_call x1, Pallas kernels, near_gradients(): pl.pallas_call(near_kernel, out_shape=(pltpu.VMEM((3, EDGE, 128, LANES),...  6.74 us
    ppermute x1, starting transfers between devices, on_device(): cross = lax.ppermute(columns, 'gx', [(1, 2), (2, 1)])  4.24 us
  transfers between devices with their start and end apart: 2, of which 1 were waited for; matrix products, arithmetic and copies ran while one was open for 0% of the time, Pallas kernels for 5%

profile of v3, /device:TPU:1, one launch (start us, length us, event | category | flops | bytes accessed | tf_op | source)
XLA Modules:
  0.0 144.9 jit_solution(4043167369828683638)
XLA Ops:
  0.0 1.6 %pack.1 = f32[32,72,128]{2,1,0:T(8,128)S(1)} custom-call(s32[1,2]{1,0:T(1,128)} %bitcast.2, f32[16,4,4096]{2,1,0:T(4,128)} %vol_ref.1), custom_call_target="tpu_custom_call" | custom-call | tf_op jit(solution)/shard_map/pack/pallas_call | solution.py:128
  1.6 27.8 %all_to_all.10.own_ref = f32[32,72,128]{2,1,0:T(8,128)S(1)} all-to-all(f32[32,72,128]{2,1,0:T(8,128)S(1)} %pack.1), channel_id=1, replica_groups=mesh['gx'=4,'dev'=32] {'dev'}, dimensions={0} | all-to-all | bytes 2359296 | tf_op jit(solution)/shard_map/all_to_all | solution.py:379
  29.4 2.1 %collective-permute-start.1 = (f32[32,72,128]{2,1,0:T(8,128)S(1)}, f32[32,72,128]{2,1,0:T(8,128)S(1)}, u32[]{:S(2)}, u32[]{:S(2)}) collective-permute-start(f32[32,72,128]{2,1,0:T(8,128)S(1)} %all_to_all.10.own_ref), channel_id=1, source_target_pairs={{0,32},{32,0},{64,96},{96,64},{1,33},{33,1},{65,97},{97,65},{2,34}... | collective-permute-start | bytes 3538952 | tf_op jit(solution)/shard_map/ppermute | solution.py:380
  31.5 4.2 %collective-permute-start = (f32[32,72,128]{2,1,0:T(8,128)S(1)}, f32[32,72,128]{2,1,0:T(8,128)S(1)}, u32[]{:S(2)}, u32[]{:S(2)}) collective-permute-start(f32[32,72,128]{2,1,0:T(8,128)S(1)} %all_to_all.10.own_ref), channel_id=1, source_target_pairs={{32,64},{64,32},{33,65},{65,33},{34,66},{66,34},{35,67},{67,35},{3... | collective-permute-start | bytes 3538952 | tf_op jit(solution)/shard_map/ppermute | solution.py:381
  35.7 0.0 collective-permute-done.1.partner_ref
  35.7 6.7 %near.1 = (f32[3,6,128,128]{3,2,1,0:T(8,128)S(1)}, f32[3,25,128,128]{3,2,1,0:T(8,128)S(1)}) custom-call(s32[1]{0:T(128)} %bitcast.place_ref, f32[32,72,128]{2,1,0:T(8,128)S(1)} %all_to_all.10.own_ref, f32[32,72,128]{2,1,0:T(8,128)S(1)} %collective-permute-done.1.partner_ref, bf16[768,256]{1,0:T(8,128)(2,1)} %constant.14.clone.g_ref, ...), custom_call_target="tpu_custom_call" | custom-call | flops 10000000000 | bytes 20000000 | tf_op jit(solution)/shard_map/near/pallas_call | solution.py:299
  42.5 8.0 %collective-permute-done.cross_ref = f32[32,72,128]{2,1,0:T(8,128)S(1)} collective-permute-done((f32[32,72,128]{2,1,0:T(8,128)S(1)}, f32[32,72,128]{2,1,0:T(8,128)S(1)}, u32[]{:S(2)}, u32[]{:S(2)}) %collective-permute-start) | collective-permute-done | bytes 1179680 | tf_op jit(solution)/shard_map/ppermute | solution.py:381
  50.5 17.8 %products.1 = f32[32,384,128]{2,1,0:T(8,128)S(1)} custom-call(s32[1]{0:T(128)} %bitcast.place_ref, f32[32,72,128]{2,1,0:T(8,128)S(1)} %collective-permute-done.cross_ref, f32[3,6,128,128]{3,2,1,0:T(8,128)S(1)} %get-tuple-element.7.edge_ref, f32[3,25,128,128]{3,2,1,0:T(8,128)S(1)} %get-tuple-element.8.near_ref, bf16[768,256]{1,0:T(8,128)(2,1)} %constant.14.clone.g_ref, ...), custom_call_target="tpu_custom_call" | custom-call | flops 10000000000 | bytes 20000000 | tf_op jit(solution)/shard_map/products/pallas_call | solution.py:315
  68.3 68.9 %all_to_all.11.in_ref = f32[32,384,128]{2,1,0:T(8,128)S(1)} all-to-all(f32[32,384,128]{2,1,0:T(8,128)S(1)} %products.1), channel_id=1, replica_groups=mesh['gx'=4,'dev'=32] {'dev'}, dimensions={0} | all-to-all | bytes 12582912 | tf_op jit(solution)/shard_map/all_to_all | solution.py:385
  137.2 7.7 %smooth_y.1 = f32[6,16,4,4096]{3,2,1,0:T(4,128)} custom-call(f32[32,384,128]{2,1,0:T(8,128)S(1)} %all_to_all.11.in_ref, bf16[1152,256]{1,0:T(8,128)(2,1)} %constant.17.clone.m_ref), custom_call_target="tpu_custom_call" | custom-call | flops 6000000000 | bytes 10000000 | tf_op jit(solution)/shard_map/smooth_y/pallas_call | solution.py:365
Async XLA Ops:
  29.4 6.3 %collective-permute-start.1 = (f32[32,72,128]{2,1,0:T(8,128)S(1)}, f32[32,72,128]{2,1,0:T(8,128)S(1)}, u32[]{:S(2)}, u32[]{:S(2)}) collective-permute-start(f32[32,72,128]{2,1,0:T(8,128)S(1)} %all_to_all.10.own_ref), channel_id=1, source_target_pairs={{0,32},{32,0},{64,96},{96,64},{1,33},{33,1},{65,97},{97,65},{2,34}... | collective-permute-start | bytes 3538952 | tf_op jit(solution)/shard_map/ppermute | solution.py:380
  31.5 19.0 %collective-permute-start = (f32[32,72,128]{2,1,0:T(8,128)S(1)}, f32[32,72,128]{2,1,0:T(8,128)S(1)}, u32[]{:S(2)}, u32[]{:S(2)}) collective-permute-start(f32[32,72,128]{2,1,0:T(8,128)S(1)} %all_to_all.10.own_ref), channel_id=1, source_target_pairs={{32,64},{64,32},{33,65},{65,33},{34,66},{66,34},{35,67},{67,35},{3... | collective-permute-start | bytes 3538952 | tf_op jit(solution)/shard_map/ppermute | solution.py:381

commit v4 on v3

--- a/solution.py
+++ b/solution.py
@@ -340,23 +340,30 @@
 GROUP = 8
 
 
+STEP = 2
+
+
 def smooth_y_kernel(in_ref, m_ref, out_ref):
     lane = lax.broadcasted_iota(jnp.int32, (64, LANES), 1)
     zero = jnp.zeros((64, LANES), F32)
-    for start in range(0, NB, 2 * GROUP):
-        stack = []
-        for j in range(start, start + 2 * GROUP, 2):
-            before = in_ref[j - 1] if j > 0 else zero
-            after = in_ref[j + 2] if j + 2 < NB else zero
-            rims = jnp.where(lane < 64, after, before)
-            xh, xl = split(jnp.concatenate([in_ref[j], in_ref[j + 1], rims], axis=1))
-            stack.append(jnp.concatenate([xh, xl, xh], axis=1))
-        o = dot(jnp.concatenate(stack, axis=0), m_ref[...])
-        for k in range(GROUP):
-            j = start + 2 * k
-            for x in range(16):
-                first = 64 * k + 4 * x
-                out_ref[0, x, :, 128 * j : 128 * j + 256] = o[first : first + 4, :]
+
+    for c in range(STEP):
+        rows = pl.ds(pl.multiple_of(64 * (2 * pl.program_id(0) + c), 64), 64)
+        for start in range(0, NB, 2 * GROUP):
+            stack = []
+            for j in range(start, start + 2 * GROUP, 2):
+                before = in_ref[j - 1, rows, :] if j > 0 else zero
+                after = in_ref[j + 2, rows, :] if j + 2 < NB else zero
+                rims = jnp.where(lane < 64, after, before)
+                pair = [in_ref[j, rows, :], in_ref[j + 1, rows, :], rims]
+                xh, xl = split(jnp.concatenate(pair, axis=1))
+                stack.append(jnp.concatenate([xh, xl, xh], axis=1))
+            o = dot(jnp.concatenate(stack, axis=0), m_ref[...])
+            for k in range(GROUP):
+                j = start + 2 * k
+                for x in range(16):
+                    first = 64 * k + 4 * x
+                    out_ref[c, x, :, 128 * j : 128 * j + 256] = o[first : first + 4, :]
 
 
 def smooth_y(received):
@@ -364,10 +371,10 @@
     m = in_hbm(np.concatenate([mh, mh, ml], axis=0))
     return pl.pallas_call(
         smooth_y_kernel,
-        grid=(6,),
+        grid=(6 // STEP,),
         out_shape=jax.ShapeDtypeStruct((6, 16, 4, NB * LANES), F32),
-        in_specs=[pl.BlockSpec((NB, 64, LANES), lambda c: (0, c, 0)), VMEM],
-        out_specs=pl.BlockSpec((1, 16, 4, NB * LANES), lambda c: (c, 0, 0, 0)),
+        in_specs=[VMEM, VMEM],
+        out_specs=pl.BlockSpec((STEP, 16, 4, NB * LANES), lambda i: (i, 0, 0, 0)),
         compiler_params=pltpu.CompilerParams(vmem_limit_bytes=24 * 2**20),
         cost_estimate=pl.CostEstimate(flops=6 * 10**9, transcendentals=0, bytes_accessed=10**7),
         name="smooth_y",

time: 145 us -> 145 us (level)
  no operation moved by 1% of the time
where the time goes in v4:
time: 145 us; the launch traced here: 144 us
  blocking collectives  96.7 us (67%)
  Pallas kernels  33.3 us (23%)
  waiting for transfers between devices  8.01 us (6%)
  starting transfers between devices  6.3 us (4%)
    all_to_all x1, blocking collectives, on_device(): received = lax.all_to_all(blocks, 'dev', 0, 0, tiled=True)  68.9 us
    all_to_all x1, blocking collectives, on_device(): columns = lax.all_to_all(message, 'dev', 0, 0, tiled=True)  27.8 us
    pallas_call x1, Pallas kernels, products(): pl.pallas_call(far_kernel, out_shape=pltpu.VMEM((NB, 384, LANES), F32), i...  17.8 us
    ppermute x1, waiting for transfers between devices, on_device(): cross = lax.ppermute(columns, 'gx', [(1, 2), (2, 1)])  8.01 us
    pallas_call x1, Pallas kernels, smooth_y(): pl.pallas_call(smooth_y_kernel, grid=(6 // STEP,), out_shape=jax.ShapeDty...  7.17 us
    pallas_call x1, Pallas kernels, near_gradients(): pl.pallas_call(near_kernel, out_shape=(pltpu.VMEM((3, EDGE, 128, LANES),...  6.74 us
    ppermute x1, starting transfers between devices, on_device(): cross = lax.ppermute(columns, 'gx', [(1, 2), (2, 1)])  4.24 us
  transfers between devices with their start and end apart: 2, of which 1 were waited for; matrix products, arithmetic and copies ran while one was open for 0% of the time, Pallas kernels for 5%

profile of v4, /device:TPU:1, one launch (start us, length us, event | category | flops | bytes accessed | tf_op | source)
XLA Modules:
  0.0 144.4 jit_solution(7688432371715374044)
XLA Ops:
  0.0 1.6 %pack.1 = f32[32,72,128]{2,1,0:T(8,128)S(1)} custom-call(s32[1,2]{1,0:T(1,128)} %bitcast.2, f32[16,4,4096]{2,1,0:T(4,128)} %vol_ref.1), custom_call_target="tpu_custom_call" | custom-call | tf_op jit(solution)/shard_map/pack/pallas_call | solution.py:128
  1.6 27.8 %all_to_all.10.own_ref = f32[32,72,128]{2,1,0:T(8,128)S(1)} all-to-all(f32[32,72,128]{2,1,0:T(8,128)S(1)} %pack.1), channel_id=1, replica_groups=mesh['gx'=4,'dev'=32] {'dev'}, dimensions={0} | all-to-all | bytes 2359296 | tf_op jit(solution)/shard_map/all_to_all | solution.py:386
  29.4 2.1 %collective-permute-start.1 = (f32[32,72,128]{2,1,0:T(8,128)S(1)}, f32[32,72,128]{2,1,0:T(8,128)S(1)}, u32[]{:S(2)}, u32[]{:S(2)}) collective-permute-start(f32[32,72,128]{2,1,0:T(8,128)S(1)} %all_to_all.10.own_ref), channel_id=1, source_target_pairs={{0,32},{32,0},{64,96},{96,64},{1,33},{33,1},{65,97},{97,65},{2,34}... | collective-permute-start | bytes 3538952 | tf_op jit(solution)/shard_map/ppermute | solution.py:387
  31.5 4.2 %collective-permute-start = (f32[32,72,128]{2,1,0:T(8,128)S(1)}, f32[32,72,128]{2,1,0:T(8,128)S(1)}, u32[]{:S(2)}, u32[]{:S(2)}) collective-permute-start(f32[32,72,128]{2,1,0:T(8,128)S(1)} %all_to_all.10.own_ref), channel_id=1, source_target_pairs={{32,64},{64,32},{33,65},{65,33},{34,66},{66,34},{35,67},{67,35},{3... | collective-permute-start | bytes 3538952 | tf_op jit(solution)/shard_map/ppermute | solution.py:388
  35.7 0.0 collective-permute-done.1.partner_ref
  35.7 6.7 %near.1 = (f32[3,6,128,128]{3,2,1,0:T(8,128)S(1)}, f32[3,25,128,128]{3,2,1,0:T(8,128)S(1)}) custom-call(s32[1]{0:T(128)} %bitcast.place_ref, f32[32,72,128]{2,1,0:T(8,128)S(1)} %all_to_all.10.own_ref, f32[32,72,128]{2,1,0:T(8,128)S(1)} %collective-permute-done.1.partner_ref, bf16[768,256]{1,0:T(8,128)(2,1)} %constant.14.clone.g_ref, ...), custom_call_target="tpu_custom_call" | custom-call | flops 10000000000 | bytes 20000000 | tf_op jit(solution)/shard_map/near/pallas_call | solution.py:299
  42.5 8.0 %collective-permute-done.cross_ref = f32[32,72,128]{2,1,0:T(8,128)S(1)} collective-permute-done((f32[32,72,128]{2,1,0:T(8,128)S(1)}, f32[32,72,128]{2,1,0:T(8,128)S(1)}, u32[]{:S(2)}, u32[]{:S(2)}) %collective-permute-start) | collective-permute-done | bytes 1179680 | tf_op jit(solution)/shard_map/ppermute | solution.py:388
  50.5 17.8 %products.1 = f32[32,384,128]{2,1,0:T(8,128)S(1)} custom-call(s32[1]{0:T(128)} %bitcast.place_ref, f32[32,72,128]{2,1,0:T(8,128)S(1)} %collective-permute-done.cross_ref, f32[3,6,128,128]{3,2,1,0:T(8,128)S(1)} %get-tuple-element.7.edge_ref, f32[3,25,128,128]{3,2,1,0:T(8,128)S(1)} %get-tuple-element.8.near_ref, bf16[768,256]{1,0:T(8,128)(2,1)} %constant.14.clone.g_ref, ...), custom_call_target="tpu_custom_call" | custom-call | flops 10000000000 | bytes 20000000 | tf_op jit(solution)/shard_map/products/pallas_call | solution.py:315
  68.3 68.9 %all_to_all.11.in_ref = f32[32,384,128]{2,1,0:T(8,128)S(1)} all-to-all(f32[32,384,128]{2,1,0:T(8,128)S(1)} %products.1), channel_id=1, replica_groups=mesh['gx'=4,'dev'=32] {'dev'}, dimensions={0} | all-to-all | bytes 12582912 | tf_op jit(solution)/shard_map/all_to_all | solution.py:392
  137.2 7.2 %smooth_y.1 = f32[6,16,4,4096]{3,2,1,0:T(4,128)} custom-call(f32[32,384,128]{2,1,0:T(8,128)S(1)} %all_to_all.11.in_ref, bf16[1152,256]{1,0:T(8,128)(2,1)} %constant.17.clone.m_ref), custom_call_target="tpu_custom_call" | custom-call | flops 6000000000 | bytes 10000000 | tf_op jit(solution)/shard_map/smooth_y/pallas_call | solution.py:372
Async XLA Ops:
  29.4 6.3 %collective-permute-start.1 = (f32[32,72,128]{2,1,0:T(8,128)S(1)}, f32[32,72,128]{2,1,0:T(8,128)S(1)}, u32[]{:S(2)}, u32[]{:S(2)}) collective-permute-start(f32[32,72,128]{2,1,0:T(8,128)S(1)} %all_to_all.10.own_ref), channel_id=1, source_target_pairs={{0,32},{32,0},{64,96},{96,64},{1,33},{33,1},{65,97},{97,65},{2,34}... | collective-permute-start | bytes 3538952 | tf_op jit(solution)/shard_map/ppermute | solution.py:387
  31.5 19.0 %collective-permute-start = (f32[32,72,128]{2,1,0:T(8,128)S(1)}, f32[32,72,128]{2,1,0:T(8,128)S(1)}, u32[]{:S(2)}, u32[]{:S(2)}) collective-permute-start(f32[32,72,128]{2,1,0:T(8,128)S(1)} %all_to_all.10.own_ref), channel_id=1, source_target_pairs={{32,64},{64,32},{33,65},{65,33},{34,66},{66,34},{35,67},{67,35},{3... | collective-permute-start | bytes 3538952 | tf_op jit(solution)/shard_map/ppermute | solution.py:388

commit v5 on v4

--- a/solution.py
+++ b/solution.py
@@ -266,7 +266,19 @@
 ):
     place = place_ref[0]
     odd = place % 2
-    line_fields(cross_ref, 32 * odd, g_ref, w_ref, fields)
+    inner = (place == 1) | (place == 2)
+
+    @pl.when(inner)
+    def _():
+        line_fields(cross_ref, 32 * odd, g_ref, w_ref, fields)
+
+    @pl.when(jnp.logical_not(inner))
+    def _():
+        zero = jnp.zeros((128, LANES), F32)
+        for f in range(3):
+            for k in range(16):
+                fields[f, 32 * odd + k] = zero
+
     for f in range(3):
         for k in range(EDGE):
             fields[f, 16 + 10 * odd + k] = edge_ref[f, k]

time: 145 us -> 143 us (0.986)
  blocking collectives: 96.7 us -> 94.8 us
    all_to_all x1, blocking collectives: 68.9 us -> 67.1 us  [on_device(): received = lax.all_to_all(blocks, 'dev', 0, 0, tiled=True)]
where the time goes in v5:
time: 143 us
  blocking collectives  94.8 us (66%)
  Pallas kernels  33.5 us (23%)
  waiting for transfers between devices  8.01 us (6%)
  starting transfers between devices  6.3 us (4%)
    all_to_all x1, blocking collectives, on_device(): received = lax.all_to_all(blocks, 'dev', 0, 0, tiled=True)  67.1 us
    all_to_all x1, blocking collectives, on_device(): columns = lax.all_to_all(message, 'dev', 0, 0, tiled=True)  27.8 us
    pallas_call x1, Pallas kernels, products(): pl.pallas_call(far_kernel, out_shape=pltpu.VMEM((NB, 384, LANES), F32), i...  18 us
    ppermute x1, waiting for transfers between devices, on_device(): cross = lax.ppermute(columns, 'gx', [(1, 2), (2, 1)])  8.01 us
    pallas_call x1, Pallas kernels, smooth_y(): pl.pallas_call(smooth_y_kernel, grid=(6 // STEP,), out_shape=jax.ShapeDty...  7.17 us
    pallas_call x1, Pallas kernels, near_gradients(): pl.pallas_call(near_kernel, out_shape=(pltpu.VMEM((3, EDGE, 128, LANES),...  6.74 us
    ppermute x1, starting transfers between devices, on_device(): cross = lax.ppermute(columns, 'gx', [(1, 2), (2, 1)])  4.24 us
  transfers between devices with their start and end apart: 2, of which 1 were waited for; matrix products, arithmetic and copies ran while one was open for 0% of the time, Pallas kernels for 5%

profile of v5, /device:TPU:1, one launch (start us, length us, event | category | flops | bytes accessed | tf_op | source)
XLA Modules:
  0.0 142.7 jit_solution(13747159170048693631)
XLA Ops:
  0.0 1.6 %pack.1 = f32[32,72,128]{2,1,0:T(8,128)S(1)} custom-call(s32[1,2]{1,0:T(1,128)} %bitcast.2, f32[16,4,4096]{2,1,0:T(4,128)} %vol_ref.1), custom_call_target="tpu_custom_call" | custom-call | tf_op jit(solution)/shard_map/pack/pallas_call | solution.py:128
  1.6 27.8 %all_to_all.10.own_ref = f32[32,72,128]{2,1,0:T(8,128)S(1)} all-to-all(f32[32,72,128]{2,1,0:T(8,128)S(1)} %pack.1), channel_id=1, replica_groups=mesh['gx'=4,'dev'=32] {'dev'}, dimensions={0} | all-to-all | bytes 2359296 | tf_op jit(solution)/shard_map/all_to_all | solution.py:398
  29.4 2.1 %collective-permute-start.1 = (f32[32,72,128]{2,1,0:T(8,128)S(1)}, f32[32,72,128]{2,1,0:T(8,128)S(1)}, u32[]{:S(2)}, u32[]{:S(2)}) collective-permute-start(f32[32,72,128]{2,1,0:T(8,128)S(1)} %all_to_all.10.own_ref), channel_id=1, source_target_pairs={{0,32},{32,0},{64,96},{96,64},{1,33},{33,1},{65,97},{97,65},{2,34}... | collective-permute-start | bytes 3538952 | tf_op jit(solution)/shard_map/ppermute | solution.py:399
  31.5 4.2 %collective-permute-start = (f32[32,72,128]{2,1,0:T(8,128)S(1)}, f32[32,72,128]{2,1,0:T(8,128)S(1)}, u32[]{:S(2)}, u32[]{:S(2)}) collective-permute-start(f32[32,72,128]{2,1,0:T(8,128)S(1)} %all_to_all.10.own_ref), channel_id=1, source_target_pairs={{32,64},{64,32},{33,65},{65,33},{34,66},{66,34},{35,67},{67,35},{3... | collective-permute-start | bytes 3538952 | tf_op jit(solution)/shard_map/ppermute | solution.py:400
  35.7 0.0 collective-permute-done.1.partner_ref
  35.7 6.7 %near.1 = (f32[3,6,128,128]{3,2,1,0:T(8,128)S(1)}, f32[3,25,128,128]{3,2,1,0:T(8,128)S(1)}) custom-call(s32[1]{0:T(128)} %bitcast.place_ref, f32[32,72,128]{2,1,0:T(8,128)S(1)} %all_to_all.10.own_ref, f32[32,72,128]{2,1,0:T(8,128)S(1)} %collective-permute-done.1.partner_ref, bf16[768,256]{1,0:T(8,128)(2,1)} %constant.14.clone.g_ref, ...), custom_call_target="tpu_custom_call" | custom-call | flops 10000000000 | bytes 20000000 | tf_op jit(solution)/shard_map/near/pallas_call | solution.py:311
  42.5 8.0 %collective-permute-done.cross_ref = f32[32,72,128]{2,1,0:T(8,128)S(1)} collective-permute-done((f32[32,72,128]{2,1,0:T(8,128)S(1)}, f32[32,72,128]{2,1,0:T(8,128)S(1)}, u32[]{:S(2)}, u32[]{:S(2)}) %collective-permute-start) | collective-permute-done | bytes 1179680 | tf_op jit(solution)/shard_map/ppermute | solution.py:400
  50.5 18.0 %products.1 = f32[32,384,128]{2,1,0:T(8,128)S(1)} custom-call(s32[1]{0:T(128)} %bitcast.place_ref, f32[32,72,128]{2,1,0:T(8,128)S(1)} %collective-permute-done.cross_ref, f32[3,6,128,128]{3,2,1,0:T(8,128)S(1)} %get-tuple-element.7.edge_ref, f32[3,25,128,128]{3,2,1,0:T(8,128)S(1)} %get-tuple-element.8.near_ref, bf16[768,256]{1,0:T(8,128)(2,1)} %constant.14.clone.g_ref, ...), custom_call_target="tpu_custom_call" | custom-call | flops 10000000000 | bytes 20000000 | tf_op jit(solution)/shard_map/products/pallas_call | solution.py:327
  68.5 67.1 %all_to_all.11.in_ref = f32[32,384,128]{2,1,0:T(8,128)S(1)} all-to-all(f32[32,384,128]{2,1,0:T(8,128)S(1)} %products.1), channel_id=1, replica_groups=mesh['gx'=4,'dev'=32] {'dev'}, dimensions={0} | all-to-all | bytes 12582912 | tf_op jit(solution)/shard_map/all_to_all | solution.py:404
  135.6 7.2 %smooth_y.1 = f32[6,16,4,4096]{3,2,1,0:T(4,128)} custom-call(f32[32,384,128]{2,1,0:T(8,128)S(1)} %all_to_all.11.in_ref, bf16[1152,256]{1,0:T(8,128)(2,1)} %constant.17.clone.m_ref), custom_call_target="tpu_custom_call" | custom-call | flops 6000000000 | bytes 10000000 | tf_op jit(solution)/shard_map/smooth_y/pallas_call | solution.py:384
Async XLA Ops:
  29.4 6.3 %collective-permute-start.1 = (f32[32,72,128]{2,1,0:T(8,128)S(1)}, f32[32,72,128]{2,1,0:T(8,128)S(1)}, u32[]{:S(2)}, u32[]{:S(2)}) collective-permute-start(f32[32,72,128]{2,1,0:T(8,128)S(1)} %all_to_all.10.own_ref), channel_id=1, source_target_pairs={{0,32},{32,0},{64,96},{96,64},{1,33},{33,1},{65,97},{97,65},{2,34}... | collective-permute-start | bytes 3538952 | tf_op jit(solution)/shard_map/ppermute | solution.py:399
  31.5 19.0 %collective-permute-start = (f32[32,72,128]{2,1,0:T(8,128)S(1)}, f32[32,72,128]{2,1,0:T(8,128)S(1)}, u32[]{:S(2)}, u32[]{:S(2)}) collective-permute-start(f32[32,72,128]{2,1,0:T(8,128)S(1)} %all_to_all.10.own_ref), channel_id=1, source_target_pairs={{32,64},{64,32},{33,65},{65,33},{34,66},{66,34},{35,67},{67,35},{3... | collective-permute-start | bytes 3538952 | tf_op jit(solution)/shard_map/ppermute | solution.py:400

commit v6 on v4

--- a/solution.py
+++ b/solution.py
@@ -266,12 +266,27 @@
 ):
     place = place_ref[0]
     odd = place % 2
-    line_fields(cross_ref, 32 * odd, g_ref, w_ref, fields)
+    inner = (place == 1) | (place == 2)
     for f in range(3):
         for k in range(EDGE):
             fields[f, 16 + 10 * odd + k] = edge_ref[f, k]
     far = NEAR * odd
-    gradient_rows(place, fields, far, FAR, grads, far, 3)
+
+    @pl.when(inner)
+    def _():
+        line_fields(cross_ref, 32 * odd, g_ref, w_ref, fields)
+        gradient_rows(place, fields, far, FAR, grads, far, 3)
+
+    @pl.when(jnp.logical_not(inner))
+    def _():
+        zero = jnp.zeros((128, LANES), F32)
+        for f in range(3):
+            for k in range(3):
+                fields[f, 13 + 19 * odd + k] = zero
+            for k in range(12):
+                grads[f, 28 * odd + k] = zero
+        start = 12 + 13 * odd
+        gradient_rows(place, fields, start, 3, grads, start, 3)
 
     def copy(i, carry):
         for f in range(3):

time: 145 us -> 144 us (level)
  no operation moved by 1% of the time
where the time goes in v6:
time: 144 us; the launch traced here: 143 us
  blocking collectives  95.3 us (66%)
  Pallas kernels  33.5 us (23%)
  waiting for transfers between devices  8.01 us (6%)
  starting transfers between devices  6.3 us (4%)
    all_to_all x1, blocking collectives, on_device(): received = lax.all_to_all(blocks, 'dev', 0, 0, tiled=True)  67.5 us
    all_to_all x1, blocking collectives, on_device(): columns = lax.all_to_all(message, 'dev', 0, 0, tiled=True)  27.8 us
    pallas_call x1, Pallas kernels, products(): pl.pallas_call(far_kernel, out_shape=pltpu.VMEM((NB, 384, LANES), F32), i...  18 us
    ppermute x1, waiting for transfers between devices, on_device(): cross = lax.ppermute(columns, 'gx', [(1, 2), (2, 1)])  8.01 us
    pallas_call x1, Pallas kernels, smooth_y(): pl.pallas_call(smooth_y_kernel, grid=(6 // STEP,), out_shape=jax.ShapeDty...  7.17 us
    pallas_call x1, Pallas kernels, near_gradients(): pl.pallas_call(near_kernel, out_shape=(pltpu.VMEM((3, EDGE, 128, LANES),...  6.74 us
    ppermute x1, starting transfers between devices, on_device(): cross = lax.ppermute(columns, 'gx', [(1, 2), (2, 1)])  4.24 us
  transfers between devices with their start and end apart: 2, of which 1 were waited for; matrix products, arithmetic and copies ran while one was open for 0% of the time, Pallas kernels for 5%

profile of v6, /device:TPU:1, one launch (start us, length us, event | category | flops | bytes accessed | tf_op | source)
XLA Modules:
  0.0 143.2 jit_solution(1739672176963508033)
XLA Ops:
  0.0 1.6 %pack.1 = f32[32,72,128]{2,1,0:T(8,128)S(1)} custom-call(s32[1,2]{1,0:T(1,128)} %bitcast.2, f32[16,4,4096]{2,1,0:T(4,128)} %vol_ref.1), custom_call_target="tpu_custom_call" | custom-call | tf_op jit(solution)/shard_map/pack/pallas_call | solution.py:128
  1.6 27.8 %all_to_all.10.own_ref = f32[32,72,128]{2,1,0:T(8,128)S(1)} all-to-all(f32[32,72,128]{2,1,0:T(8,128)S(1)} %pack.1), channel_id=1, replica_groups=mesh['gx'=4,'dev'=32] {'dev'}, dimensions={0} | all-to-all | bytes 2359296 | tf_op jit(solution)/shard_map/all_to_all | solution.py:401
  29.4 2.1 %collective-permute-start.1 = (f32[32,72,128]{2,1,0:T(8,128)S(1)}, f32[32,72,128]{2,1,0:T(8,128)S(1)}, u32[]{:S(2)}, u32[]{:S(2)}) collective-permute-start(f32[32,72,128]{2,1,0:T(8,128)S(1)} %all_to_all.10.own_ref), channel_id=1, source_target_pairs={{0,32},{32,0},{64,96},{96,64},{1,33},{33,1},{65,97},{97,65},{2,34}... | collective-permute-start | bytes 3538952 | tf_op jit(solution)/shard_map/ppermute | solution.py:402
  31.5 4.2 %collective-permute-start = (f32[32,72,128]{2,1,0:T(8,128)S(1)}, f32[32,72,128]{2,1,0:T(8,128)S(1)}, u32[]{:S(2)}, u32[]{:S(2)}) collective-permute-start(f32[32,72,128]{2,1,0:T(8,128)S(1)} %all_to_all.10.own_ref), channel_id=1, source_target_pairs={{32,64},{64,32},{33,65},{65,33},{34,66},{66,34},{35,67},{67,35},{3... | collective-permute-start | bytes 3538952 | tf_op jit(solution)/shard_map/ppermute | solution.py:403
  35.7 0.0 collective-permute-done.1.partner_ref
  35.7 6.7 %near.1 = (f32[3,6,128,128]{3,2,1,0:T(8,128)S(1)}, f32[3,25,128,128]{3,2,1,0:T(8,128)S(1)}) custom-call(s32[1]{0:T(128)} %bitcast.place_ref, f32[32,72,128]{2,1,0:T(8,128)S(1)} %all_to_all.10.own_ref, f32[32,72,128]{2,1,0:T(8,128)S(1)} %collective-permute-done.1.partner_ref, bf16[768,256]{1,0:T(8,128)(2,1)} %constant.14.clone.g_ref, ...), custom_call_target="tpu_custom_call" | custom-call | flops 10000000000 | bytes 20000000 | tf_op jit(solution)/shard_map/near/pallas_call | solution.py:314
  42.5 8.0 %collective-permute-done.cross_ref = f32[32,72,128]{2,1,0:T(8,128)S(1)} collective-permute-done((f32[32,72,128]{2,1,0:T(8,128)S(1)}, f32[32,72,128]{2,1,0:T(8,128)S(1)}, u32[]{:S(2)}, u32[]{:S(2)}) %collective-permute-start) | collective-permute-done | bytes 1179680 | tf_op jit(solution)/shard_map/ppermute | solution.py:403
  50.5 18.0 %products.1 = f32[32,384,128]{2,1,0:T(8,128)S(1)} custom-call(s32[1]{0:T(128)} %bitcast.place_ref, f32[32,72,128]{2,1,0:T(8,128)S(1)} %collective-permute-done.cross_ref, f32[3,6,128,128]{3,2,1,0:T(8,128)S(1)} %get-tuple-element.7.edge_ref, f32[3,25,128,128]{3,2,1,0:T(8,128)S(1)} %get-tuple-element.8.near_ref, bf16[768,256]{1,0:T(8,128)(2,1)} %constant.14.clone.g_ref, ...), custom_call_target="tpu_custom_call" | custom-call | flops 10000000000 | bytes 20000000 | tf_op jit(solution)/shard_map/products/pallas_call | solution.py:330
  68.5 67.5 %all_to_all.11.in_ref = f32[32,384,128]{2,1,0:T(8,128)S(1)} all-to-all(f32[32,384,128]{2,1,0:T(8,128)S(1)} %products.1), channel_id=1, replica_groups=mesh['gx'=4,'dev'=32] {'dev'}, dimensions={0} | all-to-all | bytes 12582912 | tf_op jit(solution)/shard_map/all_to_all | solution.py:407
  136.1 7.2 %smooth_y.1 = f32[6,16,4,4096]{3,2,1,0:T(4,128)} custom-call(f32[32,384,128]{2,1,0:T(8,128)S(1)} %all_to_all.11.in_ref, bf16[1152,256]{1,0:T(8,128)(2,1)} %constant.17.clone.m_ref), custom_call_target="tpu_custom_call" | custom-call | flops 6000000000 | bytes 10000000 | tf_op jit(solution)/shard_map/smooth_y/pallas_call | solution.py:387
Async XLA Ops:
  29.4 6.3 %collective-permute-start.1 = (f32[32,72,128]{2,1,0:T(8,128)S(1)}, f32[32,72,128]{2,1,0:T(8,128)S(1)}, u32[]{:S(2)}, u32[]{:S(2)}) collective-permute-start(f32[32,72,128]{2,1,0:T(8,128)S(1)} %all_to_all.10.own_ref), channel_id=1, source_target_pairs={{0,32},{32,0},{64,96},{96,64},{1,33},{33,1},{65,97},{97,65},{2,34}... | collective-permute-start | bytes 3538952 | tf_op jit(solution)/shard_map/ppermute | solution.py:402
  31.5 19.0 %collective-permute-start = (f32[32,72,128]{2,1,0:T(8,128)S(1)}, f32[32,72,128]{2,1,0:T(8,128)S(1)}, u32[]{:S(2)}, u32[]{:S(2)}) collective-permute-start(f32[32,72,128]{2,1,0:T(8,128)S(1)} %all_to_all.10.own_ref), channel_id=1, source_target_pairs={{32,64},{64,32},{33,65},{65,33},{34,66},{66,34},{35,67},{67,35},{3... | collective-permute-start | bytes 3538952 | tf_op jit(solution)/shard_map/ppermute | solution.py:403
